TPU v7x, 32 devices: a whole 2x2x4 slice. The times are simulated.
32 devices in a mesh: growth: 4 (over z), lat: 8 (over y, x, core).
Axes of the slice: x: 2, y: 2, z: 4, core: 2. Of those that a mesh axis runs over, the one named last changes fastest.
Arguments:
- source: float32 [32, 1024, 1024], P('growth', 'lat'), may hold values from -4 to 4
- spacing: float32 [32], P('growth'), may hold values from 0.5 to 2
Outputs:
- potential: float32 [32, 1024, 1024], P('growth', 'lat')
All inputs are finite; a program needn't handle non-finite values.
Results may differ from a plain program's by a relative error of at most 0.0003.
Values sent between devices are 32-bit elements; how exact they have to be, the bound alone decides.
A program may use at most 128 MiB of HBM per device.

v0:
```python
import math

import jax
import jax.numpy as jnp
from jax import lax
from jax.sharding import PartitionSpec as P

full_precision = lax.Precision.HIGHEST


def extended(cells, sides, width):
    for axis, dim in sides:
        count = lax.axis_size(axis)
        ends = count - 1
        head = lax.slice_in_dim(cells, 0, width, axis=dim)
        tail = lax.slice_in_dim(cells, cells.shape[dim] - width, cells.shape[dim], axis=dim)
        cells = jnp.concatenate(
            [
                lax.ppermute(tail, axis, [(i, (i + 1) % count) for i in range(ends)]),
                cells,
                lax.ppermute(head, axis, [((i + 1) % count, i) for i in range(ends)]),
            ],
            axis=dim,
        )
    return cells


def from_behind(array, axis, by):
    peers = lax.axis_size(axis)
    pairs = [(i, i + by) for i in range(peers) if 0 <= i + by < peers]
    return lax.ppermute(array, axis, pairs)


def cosine_table(points):
    indices = jnp.arange(points, dtype=jnp.int32)
    phase = (2 * indices[None, :] + 1) * indices[:, None] % (4 * points)
    angle = phase.astype(jnp.float32) * (math.pi / (2.0 * points))
    scale = jnp.where(indices == 0, math.sqrt(1.0 / points), math.sqrt(2.0 / points)).astype(
        jnp.float32
    )
    return scale[:, None] * jnp.cos(angle)


def mode_eigenvalue(mode_ids, points):
    sine_half = jnp.sin(mode_ids.astype(jnp.float32) * (math.pi / (2.0 * points)))
    return 4.0 * sine_half * sine_half


def tridiagonal(right_sides, lower, upper, height, eigenvalue):

    def forward(carried, row_data):
        factor, partial_value = carried
        face_below, face_above, row_height, current = row_data
        pivot = face_below + face_above + row_height * eigenvalue - face_below * factor
        factor = face_above / pivot
        partial_value = (current + face_below * partial_value) / pivot
        return ((factor, partial_value), (factor, partial_value))

    start_state = (
        jnp.zeros(eigenvalue.shape, jnp.float32),
        jnp.zeros(right_sides.shape[1:], jnp.float32),
    )
    _, (factors, partials) = lax.scan(
        forward, start_state, (lower, upper, height, right_sides), unroll=8
    )

    def backward(above_value, row_data):
        factor, partial_value = row_data
        updated = partial_value + factor * above_value
        return (updated, updated)

    _, solved = lax.scan(
        backward,
        jnp.zeros(right_sides.shape[1:], jnp.float32),
        (factors, partials),
        reverse=True,
        unroll=8,
    )
    return solved


def per_device(source, spacing):
    depth, xlocal, width_y = source.shape
    lane_count = lax.axis_size("lat")
    slab_count = lax.axis_size("growth")
    width_x = xlocal * lane_count
    table_x = cosine_table(width_x)
    table_y = cosine_table(width_y)
    lat_rank = lax.axis_index("lat")
    grow_rank = lax.axis_index("growth")
    flat_rows = source.reshape(depth * xlocal, width_y)
    planes = lax.dot_general(
        table_y,
        flat_rows,
        (((1,), (1,)), ((), ())),
        precision=full_precision,
        preferred_element_type=jnp.float32,
    )
    kx_eigen = mode_eigenvalue(jnp.arange(width_x, dtype=jnp.int32), width_x)[None, :]
    table_parts = table_x.reshape(width_x, lane_count, xlocal)
    edges = extended(spacing, (("growth", 0),), 1)
    conduct = 2.0 / (edges[:-1] + edges[1:])
    moved = lax.all_to_all(planes, "lat", split_axis=0, concat_axis=1, tiled=True)
    mode_rows = moved.shape[0]
    stacked = moved.reshape(mode_rows, lane_count, depth, xlocal)
    spectral = jnp.einsum(
        "mldx,klx->dmk",
        stacked,
        table_parts,
        precision=full_precision,
        preferred_element_type=jnp.float32,
    )
    mode_ids = lat_rank * mode_rows + jnp.arange(mode_rows, dtype=jnp.int32)
    eigenvalue = mode_eigenvalue(mode_ids, width_y)[:, None] + kx_eigen
    right_side = spacing[:, None, None] * spectral
    inner_rows = depth - 1
    row_ids = jnp.arange(inner_rows, dtype=jnp.int32)
    unit_low = jnp.where(row_ids == 0, conduct[0], 0.0)
    unit_up = jnp.where(row_ids == inner_rows - 1, conduct[inner_rows], 0.0)
    spikes = jnp.broadcast_to(
        jnp.stack([unit_low, unit_up], axis=1)[:, :, None, None],
        (inner_rows, 2, mode_rows, width_x),
    )
    right_sides = jnp.concatenate([right_side[:inner_rows, None], spikes], axis=1)
    solved = tridiagonal(
        right_sides,
        conduct[:inner_rows],
        conduct[1 : inner_rows + 1],
        spacing[:inner_rows],
        eigenvalue,
    )
    local_part = solved[:, 0]
    left_spike = solved[:, 1]
    right_spike = solved[:, 2]
    next_local, next_left, next_right = from_behind(
        (local_part[0], left_spike[0], right_spike[0]), "growth", -1
    )
    face_below = conduct[inner_rows]
    face_above = conduct[depth]
    sep_height = spacing[depth - 1]
    reduced_diag = (
        face_below
        + face_above
        + sep_height * eigenvalue
        - face_below * right_spike[inner_rows - 1]
        - face_above * next_left
    )
    reduced_sub = face_below * left_spike[inner_rows - 1]
    reduced_sup = face_above * next_right
    reduced_right = (
        right_side[depth - 1] + face_below * local_part[inner_rows - 1] + face_above * next_local
    )
    diag_all, sub_all, sup_all, right_all = (
        lax.all_gather(reduced_diag[None], "growth", axis=0, tiled=True),
        lax.all_gather(reduced_sub[None], "growth", axis=0, tiled=True),
        lax.all_gather(reduced_sup[None], "growth", axis=0, tiled=True),
        lax.all_gather(reduced_right[None], "growth", axis=0, tiled=True),
    )
    factor = jnp.zeros(eigenvalue.shape, jnp.float32)
    partial_value = jnp.zeros(eigenvalue.shape, jnp.float32)
    factors = []
    partials = []
    for slab in range(slab_count):
        pivot = diag_all[slab] - sub_all[slab] * factor
        factor = sup_all[slab] / pivot
        partial_value = (right_all[slab] + sub_all[slab] * partial_value) / pivot
        factors.append(factor)
        partials.append(partial_value)
    solutions = [partials[0]] * slab_count
    above_value = jnp.zeros(eigenvalue.shape, jnp.float32)
    for slab in reversed(range(slab_count)):
        above_value = partials[slab] + factors[slab] * above_value
        solutions[slab] = above_value
    separators = jnp.concatenate(
        [jnp.zeros((1,) + eigenvalue.shape, jnp.float32), jnp.stack(solutions)], axis=0
    )
    below_value = lax.dynamic_index_in_dim(separators, grow_rank, 0, keepdims=False)
    own_value = lax.dynamic_index_in_dim(separators, grow_rank + 1, 0, keepdims=False)
    interior = local_part + left_spike * below_value[None] + right_spike * own_value[None]
    modal = jnp.concatenate([interior, own_value[None]], axis=0)
    spatial = jnp.einsum(
        "dmk,kx->dmx", modal, table_x, precision=full_precision, preferred_element_type=jnp.float32
    )
    returned = lax.all_to_all(spatial, "lat", split_axis=2, concat_axis=1, tiled=True)
    result = jnp.einsum(
        "dyx,yw->dxw",
        returned,
        table_y,
        precision=full_precision,
        preferred_element_type=jnp.float32,
    )
    return result


def solution(mesh):
    return jax.shard_map(
        per_device,
        mesh=mesh,
        in_specs=(P("growth", "lat", None), P("growth")),
        out_specs=P("growth", "lat", None),
        check_vma=False,
    )
```

profile of v0, /device:TPU:0, one launch (start us, length us, event | category | flops | bytes accessed | tf_op | source)
XLA Modules:
  0.0 556.2 jit_solution(307421499187289886)
XLA Ops:
  6.6 34.7 %fusion.12 = f32[8,128,1024]{2,1,0:T(8,128)} fusion(f32[1024,1024,1]{1,0,2:T(8,128)} %bitcast.246, s32[8,128]{1,0:T(8,128)S(1)} %multiply_add_fusion.10, s32[1024]{0:T(1024)S(1)} %multiply_add_fusion.8, f32[8,128]{1,0:T(8,128)S(1)} %compare_select_fusion), kind=kOutput, calls=%fused_computation.34 | convolution fusion | flops 12900630528 | bytes 8400896 | tf_op jit(solution)/shard_map/dot_general | solution.py:92
  41.3 5.3 all-to-all-start
  47.3 4.9 collective-permute-start
  53.6 4.0 collective-permute-done.1
  70.3 9.1 %fusion.99 = (f32[128,1024]{0,1:T(8,128)}, f32[128,1024]{0,1:T(8,128)}, f32[128,1024]{0,1:T(8,128)}, f32[128,1024]{0,1:T(8,128)}, f32[128,1024]{0,1:T(8,128)}, /...) fusion(f32[]{:T(128)} %bitcast.14, ...), kind=kLoop, calls=%fused_computation.133 | loop fusion | flops 3276800 | bytes 5247552 | tf_op jit(solution)/shard_map/eval_jaxpr/sub | solution.py:54
  79.4 8.3 %fusion.107 = f32[128,1024]{0,1:T(8,128)} fusion(f32[]{:T(128)} %bitcast.22, f32[]{:T(128)S(6)} %add.595, f32[]{:T(128)} %bitcast.19, f32[1024]{0:T(1024)S(1)} %multiply_multiply_fusion, f32[128]{0:T(128)S(1)} %multiply_multiply_fusion.1, f32[]{:T(128)S(6)} %mul.914, f32[]{:T(128)} %bitcast.12, f32[]{:T(128)S(6)} %add.570, f32[]{:T(128)} %bitcast.11, ...), kind=kLoop, calls=%fused_computation.141 | loop fusion | flops 3801088 | bytes 528968 | tf_op jit(solution)/shard_map/eval_jaxpr/sub | solution.py:54
  87.6 8.9 %broadcast_divide_fusion = f32[128,1024]{0,1:T(8,128)} fusion(f32[]{:T(128)} %bitcast.21, f32[]{:T(128)S(6)} %mul.914, f32[]{:T(128)} %bitcast.12, f32[]{:T(128)S(6)} %add.570, f32[]{:T(128)} %bitcast.11, f32[]{:T(128)} %bitcast.14, f32[]{:T(128)S(6)} %add.579, f32[]{:T(128)} %bitcast.13, f32[]{:T(128)} %bitcast.16, f32[]{:T(128)S(6)} %add.583, ...), kind=kLoop, calls=%fused_computation.204 | loop fusion | flops 3932160 | bytes 528972 | tf_op jit(solution)/shard_map/eval_jaxpr/div | solution.py:55
  96.5 9.6 %fusion.109 = f32[128,1024]{0,1:T(8,128)} fusion(f32[]{:T(128)} %bitcast.23, f32[]{:T(128)S(6)} %add.599, f32[]{:T(128)} %bitcast.21, f32[1024]{0:T(1024)S(1)} %multiply_multiply_fusion, f32[128]{0:T(128)S(1)} %multiply_multiply_fusion.1, f32[]{:T(128)S(6)} %mul.914, f32[]{:T(128)} %bitcast.12, f32[]{:T(128)S(6)} %add.570, f32[]{:T(128)} %bitcast.11, ...), kind=kLoop, calls=%fused_computation.143 | loop fusion | flops 4456448 | bytes 528980 | tf_op jit(solution)/shard_map/eval_jaxpr/sub | solution.py:54
  106.1 10.3 %divide_multiply_fusion = f32[128,1024]{0,1:T(8,128)} fusion(f32[]{:T(128)} %bitcast.10, f32[]{:T(128)S(6)} %mul.914, f32[]{:T(128)} %bitcast.12, f32[]{:T(128)S(6)} %add.570, f32[]{:T(128)} %bitcast.11, f32[]{:T(128)} %bitcast.14, f32[]{:T(128)S(6)} %add.579, f32[]{:T(128)} %bitcast.13, f32[]{:T(128)} %bitcast.16, f32[]{:T(128)S(6)} %add.583, f32[]{:T(128)} %bitcast.15, ...), kind=kLoop, calls=%fused_computation.198 | loop fusion | flops 4718592 | bytes 528984 | tf_op jit(solution)/shard_map/eval_jaxpr/mul | solution.py:69
  116.4 46.1 %fusion.27 = f32[8,128,1024]{1,2,0:T(8,128)S(1)} fusion(s32[8,128]{1,0:T(8,128)S(1)} %multiply_add_fusion.9, f32[1024]{0:T(1024)S(1)} %fusion.138, f32[8]{0:T(128)S(1)} %copy-done.20, f32[8,128,1024]{2,1,0:T(8,128)} %all-to-all-done), kind=kOutput, calls=%fused_computation.49 | convolution fusion | flops 12901679104 | bytes 8396832 | tf_op jit(solution)/shard_map/mldx,klx->dmk/dot_general | solution.py:106
  162.7 1.8 copy-done.8
  167.6 8.2 %constant_dynamic-update-slice_fusion.3 = (f32[7,3,128,1024]{2,3,1,0:T(8,128)}, f32[1,3,128,1024]{2,3,1,0:T(8,128)}, f32[1,3,128,1024]{2,3,1,0:T(8,128)}, f32[1,...) fusion(f32[128,1024]{0,1:T(8,128)S(1)} %copy-done.5, ...), kind=kLoop, calls=%fused_computation.213 | loop fusion | flops 19267584 | bytes 30933020
  175.8 1.5 slice_multiply_fusion.1
  177.3 2.0 copy.12
  179.5 2.6 slice_bitcast_fusion.18
  185.9 31.5 %collective-permute-done.2 = f32[128,1024]{0,1:T(8,128)} collective-permute-done((f32[128,1024]{0,1:T(8,128)}, f32[128,1024]{0,1:T(8,128)}, u32[]{:S(2)}, u32[]{:S(2)}) %collective-permute-start.2) | collective-permute-done | bytes 524320 | tf_op jit(solution)/shard_map/ppermute | solution.py:31
  217.4 25.1 %collective-permute-done.3 = f32[128,1024]{0,1:T(8,128)} collective-permute-done((f32[128,1024]{0,1:T(8,128)}, f32[128,1024]{0,1:T(8,128)}, u32[]{:S(2)}, u32[]{:S(2)}) %collective-permute-start.3) | collective-permute-done | bytes 524320 | tf_op jit(solution)/shard_map/ppermute | solution.py:31
  242.5 4.5 fusion.134
  248.4 25.2 %collective-permute-done.4 = f32[128,1024]{0,1:T(8,128)S(1)} collective-permute-done((f32[128,1024]{0,1:T(8,128)}, f32[128,1024]{0,1:T(8,128)S(1)}, u32[]{:S(2)}, u32[]{:S(2)}) %collective-permute-start.4) | collective-permute-done | bytes 524320 | tf_op jit(solution)/shard_map/ppermute | solution.py:31
  276.5 3.5 fusion.137
  286.7 1.7 fusion.165
  291.6 3.9 all-gather.13.cloned.1.call-done
  295.4 49.1 %all-gather.15.cloned.1.call-done = f32[512,1024]{0,1:T(8,128)} async-done(((f32[128,1024]{0,1:T(8,128)}), f32[512,1024]{0,1:T(8,128)}) %all-gather.15.cloned.1.call-update) | async-done | bytes 2097168 | tf_op jit(solution)/shard_map/all_gather | solution.py:156
  344.5 3.0 fusion.123
  347.5 43.0 %all-gather.9.cloned.1.call-done = f32[512,1024]{0,1:T(8,128)} async-done(((f32[128,1024]{0,1:T(8,128)}), f32[512,1024]{0,1:T(8,128)}) %all-gather.9.cloned.1.call-update) | async-done | bytes 2097168 | tf_op jit(solution)/shard_map/all_gather | solution.py:157
  390.4 4.8 add_dynamic-update-slice_fusion
  399.8 30.7 %fusion.23 = f32[8,128,1024]{2,1,0:T(8,128)} fusion(f32[1,128,1024]{1,2,0:T(8,128)S(1)} %get-tuple-element.21, f32[7,128,1024]{1,2,0:T(8,128)S(1)} %fusion.43, s32[1024]{0:T(1024)S(1)} %multiply_add_fusion.8, f32[1024]{0:T(1024)S(1)} %fusion.138), kind=kOutput, calls=%fused_computation.44 | convolution fusion | flops 12901679104 | bytes 8396800 | tf_op jit(solution)/shard_map/dmk,kx->dmx/dot_general | solution.py:181
  430.5 5.4 copy.18
  435.8 52.8 %all_to_all.31 = f32[8,128,1024]{1,0,2:T(8,128)S(1)} all-to-all(f32[8,128,1024]{1,0,2:T(8,128)} %copy.18), channel_id=1, replica_groups=mesh['growth'=4,'lat'=8] {'lat'}, dimensions={2} | all-to-all | bytes 8388608 | tf_op jit(solution)/shard_map/all_to_all | solution.py:184
  488.6 4.4 copy.36
  493.0 4.9 all_to_all.28
  498.0 51.5 %fusion.36 = f32[8,128,1024]{2,1,0:T(8,128)} fusion(f32[8,1024,128]{1,2,0:T(8,128)} %all_to_all.28, s32[1024]{0:T(1024)S(1)} %multiply_add_fusion.8, f32[1024]{0:T(1024)S(1)} %fusion.138), kind=kOutput, calls=%fused_computation.57 | convolution fusion | flops 12900630528 | bytes 8396800 | tf_op jit(solution)/shard_map/dyx,yw->dxw/dot_general | solution.py:185
  (94 shorter events, 30.2 us)
Async XLA Ops:
  41.3 5.4 copy-start.20
  41.3 75.1 %all-to-all-start = ((f32[8,128,1024]{2,1,0:T(8,128)}), f32[8,128,1024]{2,1,0:T(8,128)}, u32[]{:S(2)}, u32[]{:S(2)}) async-start(f32[8,128,1024]{2,1,0:T(8,128)} %fusion.12), calls=%async_computation | async-start | bytes 8388608 | tf_op jit(solution)/shard_map/all_to_all | solution.py:103
  46.6 240.1 %all-gather.11.cloned.1.call-start = ((), (), s32[]{:S(2)}) async-start(), calls=%async_computation.3 | async-start | bytes 2621440 | tf_op jit(solution)/shard_map/all_gather | solution.py:155
  47.3 6.3 %collective-permute-start = (f32[1]{0:T(128)}, f32[1]{0:T(128)}, u32[]{:S(2)}, u32[]{:S(2)}) collective-permute-start(f32[1]{0:T(128)} %get-tuple-element.56), channel_id=1, source_target_pairs={{0,8},{8,16},{16,24},{1,9},{9,17},{17,25},{2,10},{10,18},{18,26},{... | collective-permute-start | bytes 20 | tf_op jit(solution)/shard_map/ppermute | solution.py:19
  52.2 5.4 collective-permute-start.1
  162.5 2.0 copy-start.8
  164.5 1.4 copy-start.6
  164.5 1.5 copy-start.9
  164.5 1.7 copy-start.10
  164.5 1.8 copy-start.11
  164.5 2.0 copy-start.12
  164.5 2.1 copy-start.13
  164.5 2.3 copy-start.14
  164.6 2.4 copy-start.15
  164.6 2.6 copy-start.16
  164.6 2.7 copy-start.17
  164.6 2.9 copy-start.18
  164.6 3.0 copy-start.19
  179.4 116.0 %all-gather.13.cloned.1.call-start = ((), (), s32[]{:S(2)}) async-start(), calls=%async_computation.4 | async-start | bytes 2621440 | tf_op jit(solution)/shard_map/all_gather | solution.py:154
  182.0 35.4 %collective-permute-start.2 = (f32[128,1024]{0,1:T(8,128)}, f32[128,1024]{0,1:T(8,128)}, u32[]{:S(2)}, u32[]{:S(2)}) collective-permute-start(f32[128,1024]{0,1:T(8,128)} %get-tuple-element.28), channel_id=1, source_target_pairs={{8,0},{16,8},{24,16},{9,1},{17,9},{25,17},{10,2},{18,10},{26,18},{... | collective-permute-start | bytes 1572872 | tf_op jit(solution)/shard_map/ppermute | solution.py:31
  183.3 59.2 %collective-permute-start.3 = (f32[128,1024]{0,1:T(8,128)}, f32[128,1024]{0,1:T(8,128)}, u32[]{:S(2)}, u32[]{:S(2)}) collective-permute-start(f32[128,1024]{0,1:T(8,128)} %get-tuple-element.29), channel_id=1, source_target_pairs={{8,0},{16,8},{24,16},{9,1},{17,9},{25,17},{10,2},{18,10},{26,18},{... | collective-permute-start | bytes 1572872 | tf_op jit(solution)/shard_map/ppermute | solution.py:31
  247.0 97.5 %all-gather.15.cloned.1.call-start = ((), (), s32[]{:S(2)}) async-start(), calls=%async_computation.5 | async-start | bytes 2621440 | tf_op jit(solution)/shard_map/all_gather | solution.py:156
  247.1 26.5 %collective-permute-start.4 = (f32[128,1024]{0,1:T(8,128)}, f32[128,1024]{0,1:T(8,128)S(1)}, u32[]{:S(2)}, u32[]{:S(2)}) collective-permute-start(f32[128,1024]{0,1:T(8,128)} %get-tuple-element.30), channel_id=1, source_target_pairs={{8,0},{16,8},{24,16},{9,1},{17,9},{25,17},{10,2},{18,10},{26,18},{... | collective-permute-start | bytes 1572872 | tf_op jit(solution)/shard_map/ppermute | solution.py:31
  275.0 115.4 %all-gather.9.cloned.1.call-start = ((), (), s32[]{:S(2)}) async-start(), calls=%async_computation.2 | async-start | bytes 2621440 | tf_op jit(solution)/shard_map/all_gather | solution.py:157
  275.6 4.3 copy-start
  276.5 4.8 copy-start.2
  276.5 4.8 copy-start.4
  281.2 2.7 copy-start.1
  281.2 2.7 copy-start.7
  344.5 54.6 %slice-start = ((s8[11010048]{0:T(1024)(128)(4,1)}), s8[2621440]{0:T(1024)(128)(4,1)S(1)}, s32[]{:S(2)}) async-start(s8[11010048]{0:T(1024)(128)(4,1)} %bitcast.243), calls=%async_computation.6 | async-start | bytes 5242880
  390.4 8.6 %slice-start.1 = ((s8[11010048]{0:T(1024)(128)(4,1)}), s8[4194304]{0:T(1024)(128)(4,1)S(1)}, s32[]{:S(2)}) async-start(s8[11010048]{0:T(1024)(128)(4,1)} %bitcast.243), calls=%async_computation.7 | async-start | bytes 8388608
  390.4 8.7 %slice-start.2 = ((s8[11010048]{0:T(1024)(128)(4,1)}), s8[4194304]{0:T(1024)(128)(4,1)S(1)}, s32[]{:S(2)}) async-start(s8[11010048]{0:T(1024)(128)(4,1)} %bitcast.243), calls=%async_computation.8 | async-start | bytes 8388608
  (2 other events, 2.2 us)
Sparse Core Ops, SparseCore 0:
  179.5 61.7 all-gather.10
  247.1 48.2 all-gather.12
  297.0 47.4 all-gather.14
  345.9 44.4 all-gather.8
where the time goes:
time: 556 us
  waiting for transfers between devices  182 us (33%)
  matrix products  163 us (29%)
  other arithmetic  80.3 us (14%)
  blocking collectives  52.8 us (9%)
  local copies, waits for them, and re-layouts  38.3 us (7%)
  between operations  24.1 us (4%)
  starting transfers between devices  15.5 us (3%)
    ppermute x3, waiting for transfers between devices, from_behind(): return lax.ppermute(array, axis, pairs)  81.8 us
    all_to_all x1, blocking collectives, per_device(): lax.all_to_all(spatial, 'lat', split_axis=2, concat_axis=1, tiled=True)  52.8 us
    dot_general x1, matrix products, per_device(): jnp.einsum('dyx,yw->dxw', returned, table_y, precision=full_precision, pr...  51.5 us
    all_gather x1, waiting for transfers between devices, per_device(): lax.all_gather(reduced_sup[None], 'growth', axis=0, tiled=True)  49.1 us
    dot_general x1, matrix products, per_device(): jnp.einsum('mldx,klx->dmk', stacked, table_parts, precision=full_precisio...  46.1 us
    all_gather x1, waiting for transfers between devices, per_device(): lax.all_gather(reduced_right[None], 'growth', axis=0, tiled=True)  43 us
    dot_general x1, matrix products, per_device(): lax.dot_general(table_y, flat_rows, (((1,), (1,)), ((), ())), precision=f...  34.7 us
    dot_general x1, matrix products, per_device(): jnp.einsum('dmk,kx->dmx', modal, table_x, precision=full_precision, prefe...  30.7 us
  transfers between devices with their start and end apart: 10, of which 7 were waited for; matrix products, arithmetic and copies ran while one was open for 14% of the time, Pallas kernels for 0%

commit v1 on v0

v1 whole, which is shorter than its diff:
```python
import functools
import math

import jax
import jax.numpy as jnp
import ml_dtypes
import numpy as np
from jax import lax
from jax.experimental import pallas as pl
from jax.experimental.pallas import tpu as pltpu
from jax.sharding import PartitionSpec as P

LANES = 128
PAIR = 256
MESH = pl.DeviceIdType.MESH
VMEM_BYTES = 56 * 1024 * 1024


def cosine_table(points):
    ids = np.arange(points, dtype=np.int64)
    phase = (2 * ids[None, :] + 1) * ids[:, None] % (4 * points)
    scale = np.where(ids == 0, math.sqrt(1.0 / points), math.sqrt(2.0 / points))
    return scale[:, None] * np.cos(phase * (math.pi / (2.0 * points)))


def eigenvalues(ids, points):
    return 4.0 * np.sin(np.asarray(ids) * (math.pi / (2.0 * points))) ** 2


def two_parts(table):
    high = table.astype(ml_dtypes.bfloat16)
    low = (table - high.astype(np.float64)).astype(ml_dtypes.bfloat16)
    return jnp.asarray(high), jnp.asarray(low)


def split(value):
    high = value.astype(jnp.bfloat16)
    low = (value - high.astype(jnp.float32)).astype(jnp.bfloat16)
    return high, low


def dot3(a_high, a_low, b_high, b_low):
    dot = functools.partial(jnp.dot, preferred_element_type=jnp.float32)
    return dot(a_high, b_high) + (dot(a_low, b_high) + dot(a_high, b_low))


def reciprocal(x):
    guess = pl.reciprocal(x, approx=True)
    return guess * (2.0 - x * guess)


def fill_conduct(heights_ref, cond_ref):
    heights = heights_ref[...]
    zero = jnp.zeros((1, LANES), jnp.float32)
    cond_ref[...] = 2.0 / (
        jnp.concatenate([zero, heights], axis=0) + jnp.concatenate([heights, zero], axis=0)
    )


def row(ref, z):
    return ref[pl.ds(z, 1), :]


def inverse_pivot(cond_ref, heights_ref, z, eigen, behind, face):
    diagonal = (row(cond_ref, z) + row(cond_ref, z + 1)) + row(heights_ref, z) * eigen
    return reciprocal(diagonal - (face * face) * behind)


def forward_kernel(
    slabs, lanes_count, src, spread, tyh, tyl, txh, txl, phi, lk, lb, lam,
    modal_out, jump_out, heights_out,
    heights, cond, xh, xl, f, inv_s, part_s, inv_low, inv_high, from_low, from_high,
    to_low, to_high, ends, ends_in, jumps, jumps_all, k_inv, k_part, g_modes, g_cuts,
    g_send, g_in, sem_h, sem_up, sem_down, sem_e, sem_r, sem_g,
):
    growth = lax.axis_index("growth")
    lat = lax.axis_index("lat")
    depth, m = f.shape[1], f.shape[2]
    half = m // 2
    nblk = f.shape[0]
    nz = slabs * depth
    width = src.shape[1]
    share = max(1, lanes_count // nblk)
    tiles = [slice(0, half), slice(half, m)]

    barrier = pltpu.get_barrier_semaphore()
    for off in range(1, slabs):
        pl.semaphore_signal(
            barrier, inc=1, device_id=(lax.rem(growth + off, slabs), lat), device_id_type=MESH
        )
    for off in range(1, lanes_count):
        pl.semaphore_signal(
            barrier, inc=1, device_id=(growth, lax.rem(lat + off, lanes_count)),
            device_id_type=MESH,
        )
    pl.semaphore_wait(barrier, slabs + lanes_count - 2)

    def height_copy(off, owner, target):
        return pltpu.make_async_remote_copy(
            src_ref=spread,
            dst_ref=heights.at[pl.ds(owner * depth, depth)],
            send_sem=sem_h.at[0, off],
            recv_sem=sem_h.at[1, off],
            device_id=(target, lat),
            device_id_type=MESH,
        )

    for off in range(1, slabs):
        height_copy(off, growth, lax.rem(growth + off, slabs)).start()
    heights[pl.ds(growth * depth, depth), :] = spread[...]
    rows = src.shape[0]

    def split_rows(i, carry):
        at = pl.ds(pl.multiple_of(i * m, m), m)
        high, low = split(src[at, :])
        xh[at, :] = high
        xl[at, :] = low
        return carry

    lax.fori_loop(0, depth, split_rows, 0)
    for off in range(1, slabs):
        behind = lax.rem(growth + slabs - off, slabs)
        copy = height_copy(off, behind, lax.rem(growth + off, slabs))
        copy.wait_send()
        copy.wait_recv()
    fill_conduct(heights, cond)
    heights_out[...] = heights[...]

    def eigen_of(i, tile):
        at = pl.ds(pl.multiple_of(i * LANES, LANES), LANES)
        return lk[tile, :] + lb[:, at]

    def outer_pivots(i, carry):
        eigen = [eigen_of(i, tile) for tile in tiles]
        zeros = tuple(jnp.zeros((half, LANES), jnp.float32) for _ in tiles)

        def up(z, inv):
            face = row(cond, z)
            return tuple(
                inverse_pivot(cond, heights, z, e, v, face) for e, v in zip(eigen, inv)
            )

        def down(k, inv):
            z = nz - 1 - k
            face = row(cond, z + 1)
            return tuple(
                inverse_pivot(cond, heights, z, e, v, face) for e, v in zip(eigen, inv)
            )

        low = lax.fori_loop(0, growth * depth, up, zeros)
        high = lax.fori_loop(0, nz - (growth + 1) * depth, down, zeros)
        for tile, a, b in zip(tiles, low, high):
            inv_low[i, tile, :] = a
            inv_high[i, tile, :] = b
        return carry

    lax.fori_loop(0, nblk, outer_pivots, 0)

    @pl.when(growth == 0)
    def _():
        from_low[...] = jnp.zeros_like(from_low)

    @pl.when(growth == slabs - 1)
    def _():
        from_high[...] = jnp.zeros_like(from_high)

    first = growth * depth
    chunk = min(512, rows)
    planes = chunk // m

    def transform(pair):
        columns = pl.ds(pl.multiple_of(pair * PAIR, PAIR), PAIR)

        def one(c, carry):
            at = pl.ds(pl.multiple_of(c * chunk, chunk), chunk)
            along_y = dot3(xh[at, :], xl[at, :], tyh[:, columns], tyl[:, columns])
            high, low = split(along_y)
            for k in range(planes):
                part = slice(k * m, (k + 1) * m)
                both = dot3(txh[...], txl[...], high[part, :], low[part, :])
                for side in range(PAIR // LANES):
                    f[pair * (PAIR // LANES) + side, c * planes + k] = both[
                        :, side * LANES : (side + 1) * LANES
                    ]
            return carry

        lax.fori_loop(0, rows // chunk, one, 0)

    def up_copy(i):
        return pltpu.make_async_remote_copy(
            src_ref=to_high.at[i], dst_ref=from_low.at[i],
            send_sem=sem_up.at[0, i], recv_sem=sem_up.at[1, i],
            device_id=(lax.rem(growth + 1, slabs), lat), device_id_type=MESH,
        )

    def down_copy(i):
        return pltpu.make_async_remote_copy(
            src_ref=to_low.at[i], dst_ref=from_high.at[i],
            send_sem=sem_down.at[0, i], recv_sem=sem_down.at[1, i],
            device_id=(lax.rem(growth + slabs - 1, slabs), lat), device_id_type=MESH,
        )

    def sweep_up(i):
        @pl.when(growth > 0)
        def _():
            up_copy(i).wait_recv()

        eigen = [eigen_of(i, tile) for tile in tiles]
        inv = [inv_low[i, tile, :] for tile in tiles]
        part = [from_low[i, tile, :] for tile in tiles]
        for k in range(depth):
            z = first + k
            face = row(cond, z)
            height = row(heights, z)
            for n, tile in enumerate(tiles):
                inv[n] = inverse_pivot(cond, heights, z, eigen[n], inv[n], face)
                part[n] = (height * f[i, k, tile, :] + face * part[n]) * inv[n]
                inv_s[i, k, tile, :] = inv[n]
                part_s[i, k, tile, :] = part[n]

        @pl.when(growth < slabs - 1)
        def _():
            for n, tile in enumerate(tiles):
                to_high[i, tile, :] = part[n]
            up_copy(i).start()

    def sweep_down(i):
        @pl.when(growth < slabs - 1)
        def _():
            down_copy(i).wait_recv()

        @pl.when(growth > 0)
        def _():
            eigen = [eigen_of(i, tile) for tile in tiles]
            inv = [inv_high[i, tile, :] for tile in tiles]
            part = [from_high[i, tile, :] for tile in tiles]
            for k in reversed(range(depth)):
                z = first + k
                face = row(cond, z + 1)
                height = row(heights, z)
                for n, tile in enumerate(tiles):
                    inv[n] = inverse_pivot(cond, heights, z, eigen[n], inv[n], face)
                    part[n] = (height * f[i, k, tile, :] + face * part[n]) * inv[n]
            for n, tile in enumerate(tiles):
                to_low[i, tile, :] = part[n]
            down_copy(i).start()

    def finish(i):
        face = row(cond, first + depth)
        value = []
        weight = [phi[tile, :] for tile in tiles]
        for n, tile in enumerate(tiles):
            inv = inv_s[i, depth - 1, tile, :]
            top = part_s[i, depth - 1, tile, :] + (face * inv) * from_high[i, tile, :]
            value.append(top * reciprocal(1.0 - (face * face) * inv * inv_high[i, tile, :]))
        for k in reversed(range(depth)):
            if k < depth - 1:
                face = row(cond, first + k + 1)
                for n, tile in enumerate(tiles):
                    value[n] = part_s[i, k, tile, :] + (face * inv_s[i, k, tile, :]) * value[n]
            sums = []
            for n, tile in enumerate(tiles):
                modal_out[i, k, tile, :] = value[n]
                sums.append(jnp.sum(weight[n] * value[n], axis=0, keepdims=True))
            ends[i, k : k + 1, :] = sums[0] + sums[1]
            ends[i, depth + k : depth + k + 1, :] = sums[0] - sums[1]

    per_pair = PAIR // LANES
    lag = slabs - 1

    def stage(tt, carry):
        @pl.when(tt < nblk // per_pair)
        def _():
            transform(tt)

        for side in range(per_pair):
            t = tt * per_pair + side
            up_i = t - growth
            down_i = t - (slabs - 1 - growth)
            end_i = t - lag

            @pl.when((up_i >= 0) & (up_i < nblk))
            def _():
                sweep_up(up_i)

            @pl.when((down_i >= 0) & (down_i < nblk))
            def _():
                sweep_down(down_i)

            @pl.when((end_i >= 0) & (end_i < nblk))
            def _():
                finish(end_i)

        return carry

    lax.fori_loop(0, pl.cdiv(nblk + lag, per_pair), stage, 0)

    def block_of(rank):
        return rank // share

    def ends_copy(off, owner, target):
        return pltpu.make_async_remote_copy(
            src_ref=ends.at[block_of(target)], dst_ref=ends_in.at[owner],
            send_sem=sem_e.at[0, off], recv_sem=sem_e.at[1, off],
            device_id=(growth, target), device_id_type=MESH,
        )

    for off in range(1, lanes_count):
        ends_copy(off, lat, lax.rem(lat + off, lanes_count)).start()
    ends_in[lat] = ends[block_of(lat)]

    def drain(i, carry):
        @pl.when(growth < slabs - 1)
        def _():
            up_copy(i).wait_send()

        @pl.when(growth > 0)
        def _():
            down_copy(i).wait_send()

        return carry

    lax.fori_loop(0, nblk, drain, 0)
    for off in range(1, lanes_count):
        copy = ends_copy(
            off, lax.rem(lat + lanes_count - off, lanes_count), lax.rem(lat + off, lanes_count)
        )
        copy.wait_send()
        copy.wait_recv()

    cuts = lanes_count - 1
    sines = [
        [
            math.sqrt(2.0 / lanes_count) * math.sin(math.pi * (c + 1) * (j + 1) / lanes_count)
            for j in range(cuts)
        ]
        for c in range(cuts)
    ]
    jump = [ends_in[c, depth:, :] - ends_in[c + 1, :depth, :] for c in range(cuts)]
    for j in range(cuts):
        total = jump[0] * sines[0][j]
        for c in range(1, cuts):
            total += jump[c] * sines[c][j]
        jumps[j] = total
    jumps_all[growth] = jumps[...]

    def jumps_copy(off, owner, target):
        return pltpu.make_async_remote_copy(
            src_ref=jumps, dst_ref=jumps_all.at[owner],
            send_sem=sem_r.at[0, off], recv_sem=sem_r.at[1, off],
            device_id=(target, lat), device_id_type=MESH,
        )

    for off in range(1, slabs):
        jumps_copy(off, growth, lax.rem(growth + off, slabs)).start()
    for off in range(1, slabs):
        copy = jumps_copy(
            off, lax.rem(growth + slabs - off, slabs), lax.rem(growth + off, slabs)
        )
        copy.wait_send()
        copy.wait_recv()

    block = pl.ds(pl.multiple_of(block_of(lat) * LANES, LANES), LANES)
    middle = nz // 2

    def correct(j, carry):
        def right(z):
            return row(heights, z) * jumps_all[z // depth, j, z % depth : z % depth + 1, :]

        for n, tile in enumerate(tiles):
            weight = lam[j, tile, :]
            eigen = weight + lb[:, block]
            zero = jnp.zeros((half, LANES), jnp.float32)
            inv_a, part_a, inv_b, part_b = zero, zero, zero, zero
            for k in range(middle):
                z = k
                face = row(cond, z)
                inv_a = inverse_pivot(cond, heights, z, eigen, inv_a, face)
                part_a = (right(z) + face * part_a) * inv_a
                k_inv[z] = inv_a
                k_part[z] = part_a
                z = nz - 1 - k
                face = row(cond, z + 1)
                inv_b = inverse_pivot(cond, heights, z, eigen, inv_b, face)
                part_b = (right(z) + face * part_b) * inv_b
                k_inv[z] = inv_b
                k_part[z] = part_b
            face = row(cond, middle)
            below = (part_a + (face * inv_a) * part_b) * reciprocal(
                1.0 - (face * face) * inv_a * inv_b
            )
            above = part_b + (face * inv_b) * below

            def put(z, value):
                total = jnp.sum(weight * value, axis=0, keepdims=True) * (1.0 / m)
                if n == 0:
                    held = jumps_all[z // depth, j, z % depth : z % depth + 1, :]
                else:
                    held = g_modes[j, z : z + 1, :]
                g_modes[j, z : z + 1, :] = held - total

            put(middle - 1, below)
            put(middle, above)
            for k in range(1, middle):
                z = middle - 1 - k
                below = k_part[z] + (row(cond, z + 1) * k_inv[z]) * below
                put(z, below)
                z = middle + k
                above = k_part[z] + (row(cond, z) * k_inv[z]) * above
                put(z, above)
        return carry

    lax.fori_loop(0, cuts, correct, 0)

    for c in range(cuts):
        total = g_modes[0] * sines[c][0]
        for j in range(1, cuts):
            total += g_modes[j] * sines[c][j]
        g_cuts[c] = total
    for d in range(lanes_count):
        low = g_cuts[d - 1] if d > 0 else jnp.zeros((nz, LANES), jnp.float32)
        high = g_cuts[d] if d < cuts else jnp.zeros((nz, LANES), jnp.float32)
        g_send[d, 0] = high - low
        g_send[d, 1] = -(high + low)

    def g_copy(off, owner, target):
        return pltpu.make_async_remote_copy(
            src_ref=g_send.at[target], dst_ref=g_in.at[block_of(owner)],
            send_sem=sem_g.at[0, off], recv_sem=sem_g.at[1, off],
            device_id=(growth, target), device_id_type=MESH,
        )

    def speaks(rank, act):
        if share == 1:
            act()
        else:
            pl.when(lax.rem(rank, share) == 0)(act)

    def own_block():
        g_in[block_of(lat)] = g_send[lat]

    for off in range(1, lanes_count):
        copy = g_copy(off, lat, lax.rem(lat + off, lanes_count))
        speaks(lat, copy.start)
    speaks(lat, own_block)
    for off in range(1, lanes_count):
        owner = lax.rem(lat + lanes_count - off, lanes_count)
        target = lax.rem(lat + off, lanes_count)
        speaks(lat, g_copy(off, lat, target).wait_send)
        speaks(owner, g_copy(off, owner, target).wait_recv)
    jump_out[...] = g_in[...]


def inverse_kernel(
    slabs, modal, jump, heights, tyh, tyl, txh, txl, phi, lk, lb,
    out,
    cond, inv_s, part_s, mh, ml, gh, gl,
):
    growth = lax.axis_index("growth")
    nblk, depth, m = modal.shape[:3]
    half = m // 2
    nz = slabs * depth
    tiles = [slice(0, half), slice(half, m)]
    first = growth * depth
    fill_conduct(heights, cond)
    per_pair = PAIR // LANES

    def correct(i, side):
        at = pl.ds(pl.multiple_of(i * LANES, LANES), LANES)
        eigen = [lk[tile, :] + lb[:, at] for tile in tiles]
        zero = jnp.zeros((half, LANES), jnp.float32)

        def advance(z, face, state):
            height = row(heights, z)
            new = []
            for n in range(2):
                inv, part = state[2 * n], state[2 * n + 1]
                inv = inverse_pivot(cond, heights, z, eigen[n], inv, face)
                right = height * jump[i, n, pl.ds(z, 1), :]
                new += [inv, (right + face * part) * inv]
            return tuple(new)

        def up(z, state):
            return advance(z, row(cond, z), state)

        def down(k, state):
            z = nz - 1 - k
            return advance(z, row(cond, z + 1), state)

        high = lax.fori_loop(0, nz - first - depth, down, (zero,) * 4)
        state = lax.fori_loop(0, first, up, (zero,) * 4)
        for k in range(depth):
            state = up(first + k, state)
            for n, tile in enumerate(tiles):
                inv_s[k, tile, :] = state[2 * n]
                part_s[k, tile, :] = state[2 * n + 1]
        face = row(cond, first + depth)
        value = []
        for n in range(2):
            inv, part = state[2 * n], state[2 * n + 1]
            top = part + (face * inv) * high[2 * n + 1]
            value.append(top * reciprocal(1.0 - (face * face) * inv * high[2 * n]))
        for k in reversed(range(depth)):
            if k < depth - 1:
                face = row(cond, first + k + 1)
            for n, tile in enumerate(tiles):
                if k < depth - 1:
                    value[n] = part_s[k, tile, :] + (face * inv_s[k, tile, :]) * value[n]
                a, b = split(modal[i, k, tile, :] - phi[tile, :] * value[n])
                columns = slice(side * LANES, (side + 1) * LANES)
                mh[k, tile, columns] = a
                ml[k, tile, columns] = b

    def pair(tt, carry):
        for side in range(per_pair):
            correct(tt * per_pair + side, side)
        columns = pl.ds(pl.multiple_of(tt * PAIR, PAIR), PAIR)
        for k in range(depth):
            a, b = split(dot3(txh[...], txl[...], mh[k], ml[k]))
            gh[k * m : (k + 1) * m, columns] = a
            gl[k * m : (k + 1) * m, columns] = b
        return carry

    lax.fori_loop(0, nblk // per_pair, pair, 0)

    rows = gh.shape[0]
    chunk = min(512, rows)
    width = out.shape[1]

    def columns_of(c, carry):
        columns = pl.ds(pl.multiple_of(c * PAIR, PAIR), PAIR)

        def rows_of(r, inner):
            at = pl.ds(pl.multiple_of(r * chunk, chunk), chunk)
            out[at, columns] = dot3(gh[at, :], gl[at, :], tyh[:, columns], tyl[:, columns])
            return inner

        return lax.fori_loop(0, rows // chunk, rows_of, carry)

    lax.fori_loop(0, width // PAIR, columns_of, 0)


def per_device(source, spacing):
    depth, m, width = source.shape
    lanes_count = lax.axis_size("lat")
    slabs = lax.axis_size("growth")
    nz = slabs * depth
    points = m * lanes_count
    nblk = width // LANES
    cuts = lanes_count - 1
    half = m // 2
    f32 = jnp.float32

    order = np.concatenate([np.arange(0, m, 2), np.arange(1, m, 2)])
    local = cosine_table(m)[order]
    along_y = cosine_table(width)
    tyh_t, tyl_t = two_parts(np.ascontiguousarray(along_y.T))
    tyh, tyl = two_parts(along_y)
    txh, txl = two_parts(local)
    txh_t, txl_t = two_parts(np.ascontiguousarray(local.T))

    def spread_lanes(column):
        return jnp.asarray(np.repeat(np.asarray(column, np.float32)[..., None], LANES, axis=-1))

    phi = spread_lanes(local[:, 0])
    lk = spread_lanes(eigenvalues(order, m))
    lb = jnp.asarray(eigenvalues(np.arange(width), width).astype(np.float32)[None, :])
    folds = []
    for j in range(1, lanes_count):
        ids = [k for k in range(1, points) if k % (2 * lanes_count) in (j, 2 * lanes_count - j)]
        folds.append(eigenvalues(ids, points))
    lam = spread_lanes(np.stack(folds))

    flat = source.reshape(depth * m, width)
    spread = jnp.broadcast_to(spacing[:, None], (depth, LANES))
    vmem = pl.BlockSpec(memory_space=pltpu.VMEM)
    dma = pltpu.SemaphoreType.DMA
    V = pltpu.VMEM
    modal, jump, heights = pl.pallas_call(
        functools.partial(forward_kernel, slabs, lanes_count),
        out_shape=(
            jax.ShapeDtypeStruct((nblk, depth, m, LANES), f32),
            jax.ShapeDtypeStruct((nblk, 2, nz, LANES), f32),
            jax.ShapeDtypeStruct((nz, LANES), f32),
        ),
        in_specs=[vmem] * 10,
        out_specs=(vmem, vmem, vmem),
        scratch_shapes=[
            V((nz, LANES), f32),
            V((nz + 1, LANES), f32),
            V((depth * m, width), jnp.bfloat16),
            V((depth * m, width), jnp.bfloat16),
            V((nblk, depth, m, LANES), f32),
            V((nblk, depth, m, LANES), f32),
            V((nblk, depth, m, LANES), f32),
            V((nblk, m, LANES), f32),
            V((nblk, m, LANES), f32),
            V((nblk, m, LANES), f32),
            V((nblk, m, LANES), f32),
            V((nblk, m, LANES), f32),
            V((nblk, m, LANES), f32),
            V((nblk, 2 * depth, LANES), f32),
            V((lanes_count, 2 * depth, LANES), f32),
            V((cuts, depth, LANES), f32),
            V((slabs, cuts, depth, LANES), f32),
            V((nz, half, LANES), f32),
            V((nz, half, LANES), f32),
            V((cuts, nz, LANES), f32),
            V((cuts, nz, LANES), f32),
            V((lanes_count, 2, nz, LANES), f32),
            V((nblk, 2, nz, LANES), f32),
            dma((2, slabs)),
            dma((2, nblk)),
            dma((2, nblk)),
            dma((2, lanes_count)),
            dma((2, slabs)),
            dma((2, lanes_count)),
        ],
        compiler_params=pltpu.CompilerParams(
            collective_id=0, has_side_effects=True, vmem_limit_bytes=VMEM_BYTES
        ),
        name="slab_solve",
    )(flat, spread, tyh_t, tyl_t, txh, txl, phi, lk, lb, lam)

    result = pl.pallas_call(
        functools.partial(inverse_kernel, slabs),
        out_shape=jax.ShapeDtypeStruct((depth * m, width), f32),
        in_specs=[vmem] * 10,
        out_specs=vmem,
        scratch_shapes=[
            V((nz + 1, LANES), f32),
            V((depth, m, LANES), f32),
            V((depth, m, LANES), f32),
            V((depth, m, PAIR), jnp.bfloat16),
            V((depth, m, PAIR), jnp.bfloat16),
            V((depth * m, width), jnp.bfloat16),
            V((depth * m, width), jnp.bfloat16),
        ],
        compiler_params=pltpu.CompilerParams(vmem_limit_bytes=VMEM_BYTES),
        name="face_correction",
    )(modal, jump, heights, tyh, tyl, txh_t, txl_t, phi, lk, lb)
    return result.reshape(depth, m, width)


def solution(mesh):
    return jax.shard_map(
        per_device,
        mesh=mesh,
        in_specs=(P("growth", "lat", None), P("growth")),
        out_specs=P("growth", "lat", None),
        check_vma=False,
    )
```

time: 556 us -> 107 us (0.19)
  waiting for transfers between devices: 182 us -> 0 us
  matrix products: 163 us -> 0 us
  Pallas kernels: 0 us -> 106 us
  other arithmetic: 80.3 us -> 0 us
  blocking collectives: 52.8 us -> 0 us
  local copies, waits for them, and re-layouts: 38.3 us -> 1.31 us
  between operations: 24.1 us -> 0.01 us
  starting transfers between devices: 15.5 us -> 0 us
    dot_general x4 -> x0, matrix products: 163 us -> none  [the longest x1 51.5 us: per_device(): jnp.einsum('dyx,yw->dxw', returned, table_y, precision=full_precision, pr...]
    pallas_call x0 -> x2, Pallas kernels: none -> 106 us  [the longest x1 79.7 us: per_device(): pl.pallas_call(functools.partial(forward_kernel, slabs, lanes_count), out...]
    all_gather x4 -> x0, waiting for transfers between devices: 95.9 us -> none  [the longest x1 49.1 us: per_device(): lax.all_gather(reduced_sup[None], 'growth', axis=0, tiled=True)]
    ppermute x5 -> x0, waiting for transfers between devices: 85.8 us -> none  [the longest x3 81.8 us: from_behind(): return lax.ppermute(array, axis, pairs)]
    all_to_all x1 -> x0, blocking collectives: 52.8 us -> none  [per_device(): lax.all_to_all(spatial, 'lat', split_axis=2, concat_axis=1, tiled=True)]
    sub x3 -> x0, other arithmetic: 26.9 us -> none  [forward(): face_below + face_above + row_height * eigenvalue - face_below * factor]
    unnamed x7 -> x0, other arithmetic: 20.3 us -> none
    mul x5 -> x0, other arithmetic: 13.4 us -> none  [the longest x1 10.3 us: backward(): updated = partial_value + factor * above_value]
  transfers between devices with their start and end apart: 10 -> 0, of which waited for: 7 -> 0; matrix products, arithmetic and copies ran while one was open for 14% -> 0% of each run, Pallas kernels for 0% -> 0%
where the time goes in v1:
time: 107 us
  Pallas kernels  106 us (99%)
  local copies, waits for them, and re-layouts  1.31 us (1%)
    pallas_call x1, Pallas kernels, per_device(): pl.pallas_call(functools.partial(forward_kernel, slabs, lanes_count), out...  79.7 us
    pallas_call x1, Pallas kernels, per_device(): pl.pallas_call(functools.partial(inverse_kernel, slabs), out_shape=jax.Sh...  25.8 us

profile of v1, /device:TPU:0, one launch (start us, length us, event | category | flops | bytes accessed | tf_op | source)
XLA Modules:
  0.0 106.9 jit_solution(9832202380661160259)
XLA Ops:
  0.0 1.3 %broadcast_in_dim.2.spread = f32[8,128]{1,0:T(8,128)} broadcast(f32[8]{0:T(128)} %param.15), dimensions={0} | broadcast | bytes 4128 | tf_op jit(solution)/shard_map/broadcast_in_dim | solution.py:575
  1.3 79.7 %slab_solve.1 = (f32[8,8,128,128]{3,2,1,0:T(8,128)}, f32[8,2,32,128]{3,2,1,0:T(8,128)}, f32[32,128]{1,0:T(8,128)}) custom-call(f32[1024,1024]{1,0:T(8,128)} %bitcast.2, f32[8,128]{1,0:T(8,128)} %broadcast_in_dim.2.spread, bf16[1024,1024]{1,0:T(8,128)(2,1)} %constant.24.clone.tyh, bf16[1024,1024]{1,0:T(8,128)(2,1)} %constant.25.clone.tyl, ...), custom_call_target="tpu_custom_call" | custom-call | tf_op jit(solution)/shard_map/slab_solve/pallas_call | solution.py:579
  81.1 25.8 %face_correction.1 = f32[1024,1024]{1,0:T(8,128)} custom-call(f32[8,8,128,128]{3,2,1,0:T(8,128)} %get-tuple-element.8.modal, f32[8,2,32,128]{3,2,1,0:T(8,128)} %get-tuple-element.9.jump, f32[32,128]{1,0:T(8,128)} %get-tuple-element.10.heights, bf16[1024,1024]{1,0:T(8,128)(2,1)} %constant.26.clone.tyh, bf16[1024,1024]{1,0:T(8,128)(2,1)} %constant.27.clone.tyl, ...), custom_call_target="tpu_custom_call" | custom-call | tf_op jit(solution)/shard_map/face_correction/pallas_call | solution.py:625

commit v2 on v1

--- a/solution.py
+++ b/solution.py
@@ -12,6 +12,7 @@
 
 LANES = 128
 PAIR = 256
+LAG = 2
 MESH = pl.DeviceIdType.MESH
 VMEM_BYTES = 56 * 1024 * 1024
 
@@ -67,11 +68,11 @@
 
 
 def forward_kernel(
-    slabs, lanes_count, src, spread, tyh, tyl, txh, txl, phi, lk, lb, lam,
+    slabs, lanes_count, src_in, spacing, tyh_in, tyl_in, txh, txl, phi, lk, lb, lam_in,
     modal_out, jump_out, heights_out,
-    heights, cond, xh, xl, f, inv_s, part_s, inv_low, inv_high, from_low, from_high,
+    src, spread, tyh, tyl, lam, heights, cond, xh, xl, f, inv_s, part_s, inv_high, from_low, from_high,
     to_low, to_high, ends, ends_in, jumps, jumps_all, k_inv, k_part, g_modes, g_cuts,
-    g_send, g_in, sem_h, sem_up, sem_down, sem_e, sem_r, sem_g,
+    g_send, g_in, sem_in, sem_h, sem_up, sem_down, sem_e, sem_r, sem_g,
 ):
     growth = lax.axis_index("growth")
     lat = lax.axis_index("lat")
@@ -82,6 +83,18 @@
     width = src.shape[1]
     share = max(1, lanes_count // nblk)
     tiles = [slice(0, half), slice(half, m)]
+    lag = LAG * (slabs - 1)
+
+    loads = [
+        pltpu.make_async_copy(a, b, sem_in.at[n])
+        for n, (a, b) in enumerate(
+            [(src_in, src), (tyh_in, tyh), (tyl_in, tyl), (lam_in, lam)]
+        )
+    ]
+    for load in loads:
+        load.start()
+    for k in range(depth):
+        spread[k : k + 1, :] = jnp.full((1, LANES), spacing[k], jnp.float32)
 
     barrier = pltpu.get_barrier_semaphore()
     for off in range(1, slabs):
@@ -109,6 +122,7 @@
         height_copy(off, growth, lax.rem(growth + off, slabs)).start()
     heights[pl.ds(growth * depth, depth), :] = spread[...]
     rows = src.shape[0]
+    loads[0].wait()
 
     def split_rows(i, carry):
         at = pl.ds(pl.multiple_of(i * m, m), m)
@@ -125,12 +139,14 @@
         copy.wait_recv()
     fill_conduct(heights, cond)
     heights_out[...] = heights[...]
+    for load in loads[1:]:
+        load.wait()
 
     def eigen_of(i, tile):
         at = pl.ds(pl.multiple_of(i * LANES, LANES), LANES)
         return lk[tile, :] + lb[:, at]
 
-    def outer_pivots(i, carry):
+    def pivots_below(i):
         eigen = [eigen_of(i, tile) for tile in tiles]
         zeros = tuple(jnp.zeros((half, LANES), jnp.float32) for _ in tiles)
 
@@ -139,6 +155,12 @@
             return tuple(
                 inverse_pivot(cond, heights, z, e, v, face) for e, v in zip(eigen, inv)
             )
+
+        return list(lax.fori_loop(0, growth * depth, up, zeros))
+
+    def pivots_above(i):
+        eigen = [eigen_of(i, tile) for tile in tiles]
+        zeros = tuple(jnp.zeros((half, LANES), jnp.float32) for _ in tiles)
 
         def down(k, inv):
             z = nz - 1 - k
@@ -147,14 +169,7 @@
                 inverse_pivot(cond, heights, z, e, v, face) for e, v in zip(eigen, inv)
             )
 
-        low = lax.fori_loop(0, growth * depth, up, zeros)
-        high = lax.fori_loop(0, nz - (growth + 1) * depth, down, zeros)
-        for tile, a, b in zip(tiles, low, high):
-            inv_low[i, tile, :] = a
-            inv_high[i, tile, :] = b
-        return carry
-
-    lax.fori_loop(0, nblk, outer_pivots, 0)
+        return list(lax.fori_loop(0, nz - (growth + 1) * depth, down, zeros))
 
     @pl.when(growth == 0)
     def _():
@@ -201,12 +216,13 @@
         )
 
     def sweep_up(i):
+        inv = pivots_below(i)
+
         @pl.when(growth > 0)
         def _():
             up_copy(i).wait_recv()
 
         eigen = [eigen_of(i, tile) for tile in tiles]
-        inv = [inv_low[i, tile, :] for tile in tiles]
         part = [from_low[i, tile, :] for tile in tiles]
         for k in range(depth):
             z = first + k
@@ -225,6 +241,9 @@
             up_copy(i).start()
 
     def sweep_down(i):
+        for tile, value in zip(tiles, pivots_above(i)):
+            inv_high[i, tile, :] = value
+
         @pl.when(growth < slabs - 1)
         def _():
             down_copy(i).wait_recv()
@@ -266,7 +285,25 @@
             ends[i, depth + k : depth + k + 1, :] = sums[0] - sums[1]
 
     per_pair = PAIR // LANES
-    lag = slabs - 1
+    cuts = lanes_count - 1
+    middle = nz // 2
+    per_step = pl.cdiv(cuts, lag)
+
+    def face_pivots(j):
+        weight = [lam[j, tile, :] for tile in tiles]
+        at = pl.ds(pl.multiple_of((lat // share) * LANES, LANES), LANES)
+        eigen = [w + lb[:, at] for w in weight]
+        low = [jnp.zeros((half, LANES), jnp.float32) for _ in tiles]
+        high = list(low)
+        for k in range(middle):
+            face = row(cond, k)
+            z = nz - 1 - k
+            face_high = row(cond, z + 1)
+            for n, tile in enumerate(tiles):
+                low[n] = inverse_pivot(cond, heights, k, eigen[n], low[n], face)
+                k_inv[j, k, tile, :] = low[n]
+                high[n] = inverse_pivot(cond, heights, z, eigen[n], high[n], face_high)
+                k_inv[j, z, tile, :] = high[n]
 
     def stage(tt, carry):
         @pl.when(tt < nblk // per_pair)
@@ -275,9 +312,13 @@
 
         for side in range(per_pair):
             t = tt * per_pair + side
-            up_i = t - growth
-            down_i = t - (slabs - 1 - growth)
+            up_i = t - LAG * growth
+            down_i = t - LAG * (slabs - 1 - growth)
             end_i = t - lag
+
+            for n in range(per_step):
+                j = (t - nblk) * per_step + n
+                pl.when((j >= 0) & (j < cuts))(functools.partial(face_pivots, j))
 
             @pl.when((up_i >= 0) & (up_i < nblk))
             def _():
@@ -328,7 +369,6 @@
         copy.wait_send()
         copy.wait_recv()
 
-    cuts = lanes_count - 1
     sines = [
         [
             math.sqrt(2.0 / lanes_count) * math.sin(math.pi * (c + 1) * (j + 1) / lanes_count)
@@ -360,54 +400,51 @@
         copy.wait_send()
         copy.wait_recv()
 
-    block = pl.ds(pl.multiple_of(block_of(lat) * LANES, LANES), LANES)
-    middle = nz // 2
-
     def correct(j, carry):
-        def right(z):
-            return row(heights, z) * jumps_all[z // depth, j, z % depth : z % depth + 1, :]
-
+        def held(z):
+            return jumps_all[z // depth, j, z % depth : z % depth + 1, :]
+
+        weight = [lam[j, tile, :] for tile in tiles]
+        low = [jnp.zeros((half, LANES), jnp.float32) for _ in tiles]
+        high = list(low)
+        for k in range(middle):
+            z = nz - 1 - k
+            face = row(cond, k)
+            right = row(heights, k) * held(k)
+            face_high = row(cond, z + 1)
+            right_high = row(heights, z) * held(z)
+            for n, tile in enumerate(tiles):
+                low[n] = (right + face * low[n]) * k_inv[j, k, tile, :]
+                k_part[k, tile, :] = low[n]
+                high[n] = (right_high + face_high * high[n]) * k_inv[j, z, tile, :]
+                k_part[z, tile, :] = high[n]
+
+        def put(z, value):
+            total = sum(
+                jnp.sum(w * v, axis=0, keepdims=True) for w, v in zip(weight, value)
+            )
+            g_modes[j, z : z + 1, :] = held(z) - total * (1.0 / m)
+
+        face = row(cond, middle)
+        below, above = [], []
         for n, tile in enumerate(tiles):
-            weight = lam[j, tile, :]
-            eigen = weight + lb[:, block]
-            zero = jnp.zeros((half, LANES), jnp.float32)
-            inv_a, part_a, inv_b, part_b = zero, zero, zero, zero
-            for k in range(middle):
-                z = k
-                face = row(cond, z)
-                inv_a = inverse_pivot(cond, heights, z, eigen, inv_a, face)
-                part_a = (right(z) + face * part_a) * inv_a
-                k_inv[z] = inv_a
-                k_part[z] = part_a
-                z = nz - 1 - k
-                face = row(cond, z + 1)
-                inv_b = inverse_pivot(cond, heights, z, eigen, inv_b, face)
-                part_b = (right(z) + face * part_b) * inv_b
-                k_inv[z] = inv_b
-                k_part[z] = part_b
-            face = row(cond, middle)
-            below = (part_a + (face * inv_a) * part_b) * reciprocal(
-                1.0 - (face * face) * inv_a * inv_b
-            )
-            above = part_b + (face * inv_b) * below
-
-            def put(z, value):
-                total = jnp.sum(weight * value, axis=0, keepdims=True) * (1.0 / m)
-                if n == 0:
-                    held = jumps_all[z // depth, j, z % depth : z % depth + 1, :]
-                else:
-                    held = g_modes[j, z : z + 1, :]
-                g_modes[j, z : z + 1, :] = held - total
-
-            put(middle - 1, below)
-            put(middle, above)
-            for k in range(1, middle):
-                z = middle - 1 - k
-                below = k_part[z] + (row(cond, z + 1) * k_inv[z]) * below
-                put(z, below)
-                z = middle + k
-                above = k_part[z] + (row(cond, z) * k_inv[z]) * above
-                put(z, above)
+            inv_a = face * k_inv[j, middle - 1, tile, :]
+            inv_b = face * k_inv[j, middle, tile, :]
+            below.append((low[n] + inv_a * high[n]) * reciprocal(1.0 - inv_a * inv_b))
+            above.append(high[n] + inv_b * below[n])
+        put(middle - 1, below)
+        put(middle, above)
+        for k in range(1, middle):
+            z = middle - 1 - k
+            face = row(cond, z + 1)
+            for n, tile in enumerate(tiles):
+                below[n] = k_part[z, tile, :] + (face * k_inv[j, z, tile, :]) * below[n]
+            put(z, below)
+            z = middle + k
+            face = row(cond, z)
+            for n, tile in enumerate(tiles):
+                above[n] = k_part[z, tile, :] + (face * k_inv[j, z, tile, :]) * above[n]
+            put(z, above)
         return carry
 
     lax.fori_loop(0, cuts, correct, 0)
@@ -452,18 +489,28 @@
 
 
 def inverse_kernel(
-    slabs, modal, jump, heights, tyh, tyl, txh, txl, phi, lk, lb,
-    out,
-    cond, inv_s, part_s, mh, ml, gh, gl,
+    slabs, modal_in, jump, heights, tyh_in, tyl_in, txh, txl, phi, lk, lb,
+    out_hbm,
+    modal, tyh, tyl, out, sem_in, sem_out, cond, inv_s, part_s, mh, ml, gh, gl,
 ):
     growth = lax.axis_index("growth")
     nblk, depth, m = modal.shape[:3]
+    per_pair = PAIR // LANES
+    pairs = nblk // per_pair
+    for n in range(pairs):
+        part = pl.ds(n * per_pair, per_pair)
+        pltpu.make_async_copy(modal_in.at[part], modal.at[part], sem_in.at[n]).start()
+    tables = [
+        pltpu.make_async_copy(tyh_in, tyh, sem_in.at[pairs]),
+        pltpu.make_async_copy(tyl_in, tyl, sem_in.at[pairs + 1]),
+    ]
+    for load in tables:
+        load.start()
     half = m // 2
     nz = slabs * depth
     tiles = [slice(0, half), slice(half, m)]
     first = growth * depth
     fill_conduct(heights, cond)
-    per_pair = PAIR // LANES
 
     def correct(i, side):
         at = pl.ds(pl.multiple_of(i * LANES, LANES), LANES)
@@ -512,6 +559,8 @@
                 ml[k, tile, columns] = b
 
     def pair(tt, carry):
+        part = pl.ds(tt * per_pair, per_pair)
+        pltpu.make_async_copy(modal_in.at[part], modal.at[part], sem_in.at[tt]).wait()
         for side in range(per_pair):
             correct(tt * per_pair + side, side)
         columns = pl.ds(pl.multiple_of(tt * PAIR, PAIR), PAIR)
@@ -521,7 +570,9 @@
             gl[k * m : (k + 1) * m, columns] = b
         return carry
 
-    lax.fori_loop(0, nblk // per_pair, pair, 0)
+    lax.fori_loop(0, pairs, pair, 0)
+    for load in tables:
+        load.wait()
 
     rows = gh.shape[0]
     chunk = min(512, rows)
@@ -535,9 +586,16 @@
             out[at, columns] = dot3(gh[at, :], gl[at, :], tyh[:, columns], tyl[:, columns])
             return inner
 
-        return lax.fori_loop(0, rows // chunk, rows_of, carry)
+        lax.fori_loop(0, rows // chunk, rows_of, 0)
+        store(columns, c).start()
+        return carry
+
+    def store(columns, c):
+        return pltpu.make_async_copy(out.at[:, columns], out_hbm.at[:, columns], sem_out.at[c])
 
     lax.fori_loop(0, width // PAIR, columns_of, 0)
+    for c in range(width // PAIR):
+        store(slice(c * PAIR, (c + 1) * PAIR), c).wait()
 
 
 def per_device(source, spacing):
@@ -548,7 +606,6 @@
     points = m * lanes_count
     nblk = width // LANES
     cuts = lanes_count - 1
-    half = m // 2
     f32 = jnp.float32
 
     order = np.concatenate([np.arange(0, m, 2), np.arange(1, m, 2)])
@@ -572,8 +629,9 @@
     lam = spread_lanes(np.stack(folds))
 
     flat = source.reshape(depth * m, width)
-    spread = jnp.broadcast_to(spacing[:, None], (depth, LANES))
     vmem = pl.BlockSpec(memory_space=pltpu.VMEM)
+    smem = pl.BlockSpec(memory_space=pltpu.SMEM)
+    anywhere = pl.BlockSpec(memory_space=pl.ANY)
     dma = pltpu.SemaphoreType.DMA
     V = pltpu.VMEM
     modal, jump, heights = pl.pallas_call(
@@ -583,9 +641,14 @@
             jax.ShapeDtypeStruct((nblk, 2, nz, LANES), f32),
             jax.ShapeDtypeStruct((nz, LANES), f32),
         ),
-        in_specs=[vmem] * 10,
+        in_specs=[anywhere, smem, anywhere, anywhere] + [vmem] * 5 + [anywhere],
         out_specs=(vmem, vmem, vmem),
         scratch_shapes=[
+            V((depth * m, width), f32),
+            V((depth, LANES), f32),
+            V((width, width), jnp.bfloat16),
+            V((width, width), jnp.bfloat16),
+            V((cuts, m, LANES), f32),
             V((nz, LANES), f32),
             V((nz + 1, LANES), f32),
             V((depth * m, width), jnp.bfloat16),
@@ -598,17 +661,17 @@
             V((nblk, m, LANES), f32),
             V((nblk, m, LANES), f32),
             V((nblk, m, LANES), f32),
-            V((nblk, m, LANES), f32),
             V((nblk, 2 * depth, LANES), f32),
             V((lanes_count, 2 * depth, LANES), f32),
             V((cuts, depth, LANES), f32),
             V((slabs, cuts, depth, LANES), f32),
-            V((nz, half, LANES), f32),
-            V((nz, half, LANES), f32),
+            V((cuts, nz, m, LANES), f32),
+            V((nz, m, LANES), f32),
             V((cuts, nz, LANES), f32),
             V((cuts, nz, LANES), f32),
             V((lanes_count, 2, nz, LANES), f32),
             V((nblk, 2, nz, LANES), f32),
+            dma((4,)),
             dma((2, slabs)),
             dma((2, nblk)),
             dma((2, nblk)),
@@ -620,14 +683,20 @@
             collective_id=0, has_side_effects=True, vmem_limit_bytes=VMEM_BYTES
         ),
         name="slab_solve",
-    )(flat, spread, tyh_t, tyl_t, txh, txl, phi, lk, lb, lam)
+    )(flat, spacing, tyh_t, tyl_t, txh, txl, phi, lk, lb, lam)
 
     result = pl.pallas_call(
         functools.partial(inverse_kernel, slabs),
         out_shape=jax.ShapeDtypeStruct((depth * m, width), f32),
-        in_specs=[vmem] * 10,
-        out_specs=vmem,
+        in_specs=[anywhere, vmem, vmem, anywhere, anywhere] + [vmem] * 5,
+        out_specs=anywhere,
         scratch_shapes=[
+            V((nblk, depth, m, LANES), f32),
+            V((width, width), jnp.bfloat16),
+            V((width, width), jnp.bfloat16),
+            V((depth * m, width), f32),
+            dma((width // PAIR + 2,)),
+            dma((width // PAIR,)),
             V((nz + 1, LANES), f32),
             V((depth, m, LANES), f32),
             V((depth, m, LANES), f32),

time: 107 us -> 83.7 us (0.78)
  Pallas kernels: 106 us -> 83.5 us
  local copies, waits for them, and re-layouts: 1.31 us -> 0 us
    pallas_call x1, Pallas kernels: 79.7 us -> 60 us  [per_device(): pl.pallas_call(functools.partial(forward_kernel, slabs, lanes_count), out...]
    pallas_call x1, Pallas kernels: 25.8 us -> 23.5 us  [per_device(): pl.pallas_call(functools.partial(inverse_kernel, slabs), out_shape=jax.Sh...]
    broadcast_in_dim x1 -> x0, local copies, waits for them, and re-layouts: 1.31 us -> none  [per_device(): spread = jnp.broadcast_to(spacing[:, None], (depth, LANES))]
where the time goes in v2:
time: 83.7 us; the launch traced here: 83.5 us
  Pallas kernels  83.5 us (100%)
    pallas_call x1, Pallas kernels, per_device(): pl.pallas_call(functools.partial(forward_kernel, slabs, lanes_count), out...  60 us
    pallas_call x1, Pallas kernels, per_device(): pl.pallas_call(functools.partial(inverse_kernel, slabs), out_shape=jax.Sh...  23.5 us

profile of v2, /device:TPU:0, one launch (start us, length us, event | category | flops | bytes accessed | tf_op | source)
XLA Modules:
  0.0 83.5 jit_solution(13268084512299415061)
XLA Ops:
  0.0 60.0 %slab_solve.1 = (f32[8,8,128,128]{3,2,1,0:T(8,128)}, f32[8,2,32,128]{3,2,1,0:T(8,128)}, f32[32,128]{1,0:T(8,128)}) custom-call(f32[1024,1024]{1,0:T(8,128)} %bitcast.2, f32[8]{0:T(128)} %spacing.1, bf16[1024,1024]{1,0:T(8,128)(2,1)} %constant.24.clone.tyh_in, bf16[1024,1024]{1,0:T(8,128)(2,1)} %constant.25.clone.tyl_in, ...), custom_call_target="tpu_custom_call" | custom-call | tf_op jit(solution)/shard_map/slab_solve/pallas_call | solution.py:637
  60.1 23.5 %face_correction.1 = f32[1024,1024]{1,0:T(8,128)} custom-call(f32[8,8,128,128]{3,2,1,0:T(8,128)} %get-tuple-element.8.modal_in, f32[8,2,32,128]{3,2,1,0:T(8,128)} %get-tuple-element.9.jump, f32[32,128]{1,0:T(8,128)} %get-tuple-element.10.heights, bf16[1024,1024]{1,0:T(8,128)(2,1)} %constant.26.clone.tyh_in, bf16[1024,1024]{1,0:T(8,128)(2,1)} %constant.27.clone.tyl_in, ...), custom_call_target="tpu_custom_call" | custom-call | tf_op jit(solution)/shard_map/face_correction/pallas_call | solution.py:688

commit v3 on v2

--- a/solution.py
+++ b/solution.py
@@ -31,7 +31,22 @@
 def two_parts(table):
     high = table.astype(ml_dtypes.bfloat16)
     low = (table - high.astype(np.float64)).astype(ml_dtypes.bfloat16)
-    return jnp.asarray(high), jnp.asarray(low)
+    return high, low
+
+
+def left_parts(table):
+    high, low = two_parts(table)
+    return jnp.asarray(np.concatenate([high, low, high], axis=-1))
+
+
+def right_parts(table):
+    high, low = two_parts(table)
+    return jnp.asarray(np.concatenate([high, high, low], axis=-2))
+
+
+def mirror(value):
+    lanes = lax.broadcasted_iota(jnp.int32, value.shape, 1)
+    return jnp.take_along_axis(value, LANES - 1 - lanes, axis=1, mode="promise_in_bounds")
 
 
 def split(value):
@@ -40,9 +55,13 @@
     return high, low
 
 
-def dot3(a_high, a_low, b_high, b_low):
-    dot = functools.partial(jnp.dot, preferred_element_type=jnp.float32)
-    return dot(a_high, b_high) + (dot(a_low, b_high) + dot(a_high, b_low))
+def dot(a, b):
+    return jnp.dot(a, b, preferred_element_type=jnp.float32)
+
+
+def stacked(value):
+    high, low = split(value)
+    return jnp.concatenate([high, high, low], axis=0)
 
 
 def reciprocal(x):
@@ -68,9 +87,9 @@
 
 
 def forward_kernel(
-    slabs, lanes_count, src_in, spacing, tyh_in, tyl_in, txh, txl, phi, lk, lb, lam_in,
+    slabs, lanes_count, src_in, spacing, ty_in, tx, phi, lk, lb, lam_in,
     modal_out, jump_out, heights_out,
-    src, spread, tyh, tyl, lam, heights, cond, xh, xl, f, inv_s, part_s, inv_high, from_low, from_high,
+    src, spread, ty, lam, heights, cond, x3, f, inv_s, part_s, inv_high, from_low, from_high,
     to_low, to_high, ends, ends_in, jumps, jumps_all, k_inv, k_part, g_modes, g_cuts,
     g_send, g_in, sem_in, sem_h, sem_up, sem_down, sem_e, sem_r, sem_g,
 ):
@@ -88,7 +107,7 @@
     loads = [
         pltpu.make_async_copy(a, b, sem_in.at[n])
         for n, (a, b) in enumerate(
-            [(src_in, src), (tyh_in, tyh), (tyl_in, tyl), (lam_in, lam)]
+            [(src_in, src), (ty_in, ty), (lam_in, lam)]
         )
     ]
     for load in loads:
@@ -124,11 +143,18 @@
     rows = src.shape[0]
     loads[0].wait()
 
+    mid = width // 2
+
     def split_rows(i, carry):
         at = pl.ds(pl.multiple_of(i * m, m), m)
-        high, low = split(src[at, :])
-        xh[at, :] = high
-        xl[at, :] = low
+        for q in range(mid // LANES):
+            near = src[at, q * LANES : (q + 1) * LANES]
+            far = mirror(src[at, width - (q + 1) * LANES : width - q * LANES])
+            for n, value in enumerate((near + far, near - far)):
+                high, low = split(value)
+                for place, part in enumerate((high, low, high)):
+                    start = place * mid + q * LANES
+                    x3[n, at, start : start + LANES] = part
         return carry
 
     lax.fori_loop(0, depth, split_rows, 0)
@@ -183,16 +209,18 @@
     chunk = min(512, rows)
     planes = chunk // m
 
+    half_pairs = mid // PAIR
+
     def transform(pair):
-        columns = pl.ds(pl.multiple_of(pair * PAIR, PAIR), PAIR)
+        parity = pair // half_pairs
+        columns = pl.ds(pl.multiple_of(lax.rem(pair, half_pairs) * PAIR, PAIR), PAIR)
 
         def one(c, carry):
             at = pl.ds(pl.multiple_of(c * chunk, chunk), chunk)
-            along_y = dot3(xh[at, :], xl[at, :], tyh[:, columns], tyl[:, columns])
-            high, low = split(along_y)
+            along_y = dot(x3[parity, at, :], ty[parity, :, columns])
             for k in range(planes):
                 part = slice(k * m, (k + 1) * m)
-                both = dot3(txh[...], txl[...], high[part, :], low[part, :])
+                both = dot(tx[...], stacked(along_y[part, :]))
                 for side in range(PAIR // LANES):
                     f[pair * (PAIR // LANES) + side, c * planes + k] = both[
                         :, side * LANES : (side + 1) * LANES
@@ -489,9 +517,9 @@
 
 
 def inverse_kernel(
-    slabs, modal_in, jump, heights, tyh_in, tyl_in, txh, txl, phi, lk, lb,
+    slabs, modal_in, jump, heights, ty_in, tx, phi, lk, lb,
     out_hbm,
-    modal, tyh, tyl, out, sem_in, sem_out, cond, inv_s, part_s, mh, ml, gh, gl,
+    modal, ty, out, sem_in, sem_out, cond, inv_s, part_s, m3, g3,
 ):
     growth = lax.axis_index("growth")
     nblk, depth, m = modal.shape[:3]
@@ -500,12 +528,8 @@
     for n in range(pairs):
         part = pl.ds(n * per_pair, per_pair)
         pltpu.make_async_copy(modal_in.at[part], modal.at[part], sem_in.at[n]).start()
-    tables = [
-        pltpu.make_async_copy(tyh_in, tyh, sem_in.at[pairs]),
-        pltpu.make_async_copy(tyl_in, tyl, sem_in.at[pairs + 1]),
-    ]
-    for load in tables:
-        load.start()
+    table = pltpu.make_async_copy(ty_in, ty, sem_in.at[pairs])
+    table.start()
     half = m // 2
     nz = slabs * depth
     tiles = [slice(0, half), slice(half, m)]
@@ -555,47 +579,64 @@
                     value[n] = part_s[k, tile, :] + (face * inv_s[k, tile, :]) * value[n]
                 a, b = split(modal[i, k, tile, :] - phi[tile, :] * value[n])
                 columns = slice(side * LANES, (side + 1) * LANES)
-                mh[k, tile, columns] = a
-                ml[k, tile, columns] = b
+                for place, part in enumerate((a, a, b)):
+                    start = place * m + n * half
+                    m3[k, start : start + half, columns] = part
 
     def pair(tt, carry):
         part = pl.ds(tt * per_pair, per_pair)
         pltpu.make_async_copy(modal_in.at[part], modal.at[part], sem_in.at[tt]).wait()
         for side in range(per_pair):
             correct(tt * per_pair + side, side)
-        columns = pl.ds(pl.multiple_of(tt * PAIR, PAIR), PAIR)
+        parity = tt // half_pairs
+        offset = lax.rem(tt, half_pairs) * PAIR
         for k in range(depth):
-            a, b = split(dot3(txh[...], txl[...], mh[k], ml[k]))
-            gh[k * m : (k + 1) * m, columns] = a
-            gl[k * m : (k + 1) * m, columns] = b
+            a, b = split(dot(tx[...], m3[k]))
+            for place, part in enumerate((a, b, a)):
+                columns = pl.ds(pl.multiple_of(place * mid + offset, PAIR), PAIR)
+                g3[parity, k * m : (k + 1) * m, columns] = part
         return carry
 
+    width = out.shape[1]
+    mid = width // 2
+    half_pairs = mid // PAIR
+
     lax.fori_loop(0, pairs, pair, 0)
-    for load in tables:
-        load.wait()
-
-    rows = gh.shape[0]
-    chunk = min(512, rows)
-    width = out.shape[1]
+    table.wait()
+
+    rows = out.shape[0]
+    chunk = min(256, rows)
+
+    def store(c, side):
+        start = c * PAIR if side == 0 else width - (c + 1) * PAIR
+        columns = pl.ds(start if isinstance(c, int) else pl.multiple_of(start, PAIR), PAIR)
+        return pltpu.make_async_copy(
+            out.at[:, columns], out_hbm.at[:, columns], sem_out.at[2 * c + side]
+        )
 
     def columns_of(c, carry):
         columns = pl.ds(pl.multiple_of(c * PAIR, PAIR), PAIR)
 
         def rows_of(r, inner):
             at = pl.ds(pl.multiple_of(r * chunk, chunk), chunk)
-            out[at, columns] = dot3(gh[at, :], gl[at, :], tyh[:, columns], tyl[:, columns])
+            even = dot(g3[0, at, :], ty[0, :, columns])
+            odd = dot(g3[1, at, :], ty[1, :, columns])
+            out[at, columns] = even + odd
+            far = even - odd
+            for q in range(PAIR // LANES):
+                start = pl.multiple_of(width - c * PAIR - (q + 1) * LANES, LANES)
+                out[at, pl.ds(start, LANES)] = mirror(far[:, q * LANES : (q + 1) * LANES])
             return inner
 
         lax.fori_loop(0, rows // chunk, rows_of, 0)
-        store(columns, c).start()
+        for side in range(2):
+            store(c, side).start()
         return carry
 
-    def store(columns, c):
-        return pltpu.make_async_copy(out.at[:, columns], out_hbm.at[:, columns], sem_out.at[c])
-
-    lax.fori_loop(0, width // PAIR, columns_of, 0)
-    for c in range(width // PAIR):
-        store(slice(c * PAIR, (c + 1) * PAIR), c).wait()
+    lax.fori_loop(0, half_pairs, columns_of, 0)
+    for c in range(half_pairs):
+        for side in range(2):
+            store(c, side).wait()
 
 
 def per_device(source, spacing):
@@ -610,18 +651,21 @@
 
     order = np.concatenate([np.arange(0, m, 2), np.arange(1, m, 2)])
     local = cosine_table(m)[order]
+    mid = width // 2
     along_y = cosine_table(width)
-    tyh_t, tyl_t = two_parts(np.ascontiguousarray(along_y.T))
-    tyh, tyl = two_parts(along_y)
-    txh, txl = two_parts(local)
-    txh_t, txl_t = two_parts(np.ascontiguousarray(local.T))
+    halves = np.stack([along_y[0::2, :mid], along_y[1::2, :mid]])
+    ty_forward = right_parts(np.swapaxes(halves, 1, 2))
+    ty_back = right_parts(halves)
+    tx_forward = left_parts(local)
+    tx_back = left_parts(local.T)
+    mode_y = np.concatenate([np.arange(0, width, 2), np.arange(1, width, 2)])
 
     def spread_lanes(column):
         return jnp.asarray(np.repeat(np.asarray(column, np.float32)[..., None], LANES, axis=-1))
 
     phi = spread_lanes(local[:, 0])
     lk = spread_lanes(eigenvalues(order, m))
-    lb = jnp.asarray(eigenvalues(np.arange(width), width).astype(np.float32)[None, :])
+    lb = jnp.asarray(eigenvalues(mode_y, width).astype(np.float32)[None, :])
     folds = []
     for j in range(1, lanes_count):
         ids = [k for k in range(1, points) if k % (2 * lanes_count) in (j, 2 * lanes_count - j)]
@@ -641,18 +685,16 @@
             jax.ShapeDtypeStruct((nblk, 2, nz, LANES), f32),
             jax.ShapeDtypeStruct((nz, LANES), f32),
         ),
-        in_specs=[anywhere, smem, anywhere, anywhere] + [vmem] * 5 + [anywhere],
+        in_specs=[anywhere, smem, anywhere] + [vmem] * 4 + [anywhere],
         out_specs=(vmem, vmem, vmem),
         scratch_shapes=[
             V((depth * m, width), f32),
             V((depth, LANES), f32),
-            V((width, width), jnp.bfloat16),
-            V((width, width), jnp.bfloat16),
+            V((2, 3 * mid, mid), jnp.bfloat16),
             V((cuts, m, LANES), f32),
             V((nz, LANES), f32),
             V((nz + 1, LANES), f32),
-            V((depth * m, width), jnp.bfloat16),
-            V((depth * m, width), jnp.bfloat16),
+            V((2, depth * m, 3 * mid), jnp.bfloat16),
             V((nblk, depth, m, LANES), f32),
             V((nblk, depth, m, LANES), f32),
             V((nblk, depth, m, LANES), f32),
@@ -671,7 +713,7 @@
             V((cuts, nz, LANES), f32),
             V((lanes_count, 2, nz, LANES), f32),
             V((nblk, 2, nz, LANES), f32),
-            dma((4,)),
+            dma((3,)),
             dma((2, slabs)),
             dma((2, nblk)),
             dma((2, nblk)),
@@ -683,31 +725,28 @@
             collective_id=0, has_side_effects=True, vmem_limit_bytes=VMEM_BYTES
         ),
         name="slab_solve",
-    )(flat, spacing, tyh_t, tyl_t, txh, txl, phi, lk, lb, lam)
+    )(flat, spacing, ty_forward, tx_forward, phi, lk, lb, lam)
 
     result = pl.pallas_call(
         functools.partial(inverse_kernel, slabs),
         out_shape=jax.ShapeDtypeStruct((depth * m, width), f32),
-        in_specs=[anywhere, vmem, vmem, anywhere, anywhere] + [vmem] * 5,
+        in_specs=[anywhere, vmem, vmem, anywhere] + [vmem] * 4,
         out_specs=anywhere,
         scratch_shapes=[
             V((nblk, depth, m, LANES), f32),
-            V((width, width), jnp.bfloat16),
-            V((width, width), jnp.bfloat16),
+            V((2, 3 * mid, mid), jnp.bfloat16),
             V((depth * m, width), f32),
             dma((width // PAIR + 2,)),
             dma((width // PAIR,)),
             V((nz + 1, LANES), f32),
             V((depth, m, LANES), f32),
             V((depth, m, LANES), f32),
-            V((depth, m, PAIR), jnp.bfloat16),
-            V((depth, m, PAIR), jnp.bfloat16),
-            V((depth * m, width), jnp.bfloat16),
-            V((depth * m, width), jnp.bfloat16),
+            V((depth, 3 * m, PAIR), jnp.bfloat16),
+            V((2, depth * m, 3 * mid), jnp.bfloat16),
         ],
         compiler_params=pltpu.CompilerParams(vmem_limit_bytes=VMEM_BYTES),
         name="face_correction",
-    )(modal, jump, heights, tyh, tyl, txh_t, txl_t, phi, lk, lb)
+    )(modal, jump, heights, ty_back, tx_back, phi, lk, lb)
     return result.reshape(depth, m, width)
 
 

time: 83.7 us -> 78.2 us (0.934)
  Pallas kernels: 83.5 us -> 78 us
    pallas_call x1, Pallas kernels: 60 us -> 57.2 us  [per_device(): pl.pallas_call(functools.partial(forward_kernel, slabs, lanes_count), out...]
    pallas_call x1, Pallas kernels: 23.5 us -> 20.8 us  [per_device(): pl.pallas_call(functools.partial(inverse_kernel, slabs), out_shape=jax.Sh...]
where the time goes in v3:
time: 78.2 us; the launch traced here: 78.1 us
  Pallas kernels  78 us (100%)
    pallas_call x1, Pallas kernels, per_device(): pl.pallas_call(functools.partial(forward_kernel, slabs, lanes_count), out...  57.2 us
    pallas_call x1, Pallas kernels, per_device(): pl.pallas_call(functools.partial(inverse_kernel, slabs), out_shape=jax.Sh...  20.8 us

profile of v3, /device:TPU:0, one launch (start us, length us, event | category | flops | bytes accessed | tf_op | source)
XLA Modules:
  0.0 78.1 jit_solution(13263330527558861472)
XLA Ops:
  0.0 57.2 %slab_solve.1 = (f32[8,8,128,128]{3,2,1,0:T(8,128)}, f32[8,2,32,128]{3,2,1,0:T(8,128)}, f32[32,128]{1,0:T(8,128)}) custom-call(f32[1024,1024]{1,0:T(8,128)} %bitcast.2, f32[8]{0:T(128)} %spacing.1, bf16[2,1536,512]{2,1,0:T(8,128)(2,1)} %constant.16.clone.ty_in, bf16[128,384]{1,0:T(8,128)(2,1)} %constant.18.clone.tx, f32[128,128]{1,0:T(8,128)} %constant.20.clone.phi, ...), custom_call_target="tpu_custom_call" | custom-call | tf_op jit(solution)/shard_map/slab_solve/pallas_call | solution.py:681
  57.2 20.8 %face_correction.1 = f32[1024,1024]{1,0:T(8,128)} custom-call(f32[8,8,128,128]{3,2,1,0:T(8,128)} %get-tuple-element.8.modal_in, f32[8,2,32,128]{3,2,1,0:T(8,128)} %get-tuple-element.9.jump, f32[32,128]{1,0:T(8,128)} %get-tuple-element.10.heights, bf16[2,1536,512]{2,1,0:T(8,128)(2,1)} %constant.17.clone.ty_in, bf16[128,384]{1,0:T(8,128)(2,1)} %constant.19.clone.tx, ...), custom_call_target="tpu_custom_call" | custom-call | tf_op jit(solution)/shard_map/face_correction/pallas_call | solution.py:730

commit v4 on v3

--- a/solution.py
+++ b/solution.py
@@ -86,12 +86,28 @@
     return reciprocal(diagonal - (face * face) * behind)
 
 
+def leap(cond_ref, heights_ref, first, depth, eigen, inv, part, right, upward):
+    newest, before = None, inv
+    for k in range(depth):
+        z = first + (k if upward else depth - 1 - k)
+        face = row(cond_ref, z if upward else z + 1)
+        diagonal = (row(cond_ref, z) + row(cond_ref, z + 1)) + row(heights_ref, z) * eigen
+        if newest is None:
+            part = right(z) + face * part if right else None
+            newest, before = diagonal - (face * face) * before, 1.0
+        else:
+            part = right(z) * newest + face * part if right else None
+            newest, before = diagonal * newest - (face * face) * before, newest
+    scale = reciprocal(newest)
+    return before * scale, part * scale if right else None
+
+
 def forward_kernel(
     slabs, lanes_count, src_in, spacing, ty_in, tx, phi, lk, lb, lam_in,
     modal_out, jump_out, heights_out,
-    src, spread, ty, lam, heights, cond, x3, f, inv_s, part_s, inv_high, from_low, from_high,
+    modal, src, spread, ty, lam, heights, cond, x3, f, inv_s, part_s, inv_high, from_low, from_high,
     to_low, to_high, ends, ends_in, jumps, jumps_all, k_inv, k_part, g_modes, g_cuts,
-    g_send, g_in, sem_in, sem_h, sem_up, sem_down, sem_e, sem_r, sem_g,
+    g_send, g_in, sem_in, sem_m, sem_h, sem_up, sem_down, sem_e, sem_r, sem_g,
 ):
     growth = lax.axis_index("growth")
     lat = lax.axis_index("lat")
@@ -173,29 +189,30 @@
         return lk[tile, :] + lb[:, at]
 
     def pivots_below(i):
-        eigen = [eigen_of(i, tile) for tile in tiles]
-        zeros = tuple(jnp.zeros((half, LANES), jnp.float32) for _ in tiles)
-
-        def up(z, inv):
-            face = row(cond, z)
-            return tuple(
-                inverse_pivot(cond, heights, z, e, v, face) for e, v in zip(eigen, inv)
+        def one(tile):
+            eigen = eigen_of(i, tile)
+            return lax.fori_loop(
+                0, growth,
+                lambda n, inv: leap(
+                    cond, heights, n * depth, depth, eigen, inv, None, None, True
+                )[0],
+                jnp.zeros((half, LANES), jnp.float32),
             )
 
-        return list(lax.fori_loop(0, growth * depth, up, zeros))
+        return [one(tile) for tile in tiles]
 
     def pivots_above(i):
-        eigen = [eigen_of(i, tile) for tile in tiles]
-        zeros = tuple(jnp.zeros((half, LANES), jnp.float32) for _ in tiles)
-
-        def down(k, inv):
-            z = nz - 1 - k
-            face = row(cond, z + 1)
-            return tuple(
-                inverse_pivot(cond, heights, z, e, v, face) for e, v in zip(eigen, inv)
+        def one(tile):
+            eigen = eigen_of(i, tile)
+            return lax.fori_loop(
+                0, slabs - 1 - growth,
+                lambda n, inv: leap(
+                    cond, heights, (slabs - 1 - n) * depth, depth, eigen, inv, None, None, False
+                )[0],
+                jnp.zeros((half, LANES), jnp.float32),
             )
 
-        return list(lax.fori_loop(0, nz - (growth + 1) * depth, down, zeros))
+        return [one(tile) for tile in tiles]
 
     @pl.when(growth == 0)
     def _():
@@ -278,19 +295,27 @@
 
         @pl.when(growth > 0)
         def _():
-            eigen = [eigen_of(i, tile) for tile in tiles]
-            inv = [inv_high[i, tile, :] for tile in tiles]
-            part = [from_high[i, tile, :] for tile in tiles]
-            for k in reversed(range(depth)):
-                z = first + k
-                face = row(cond, z + 1)
-                height = row(heights, z)
-                for n, tile in enumerate(tiles):
-                    inv[n] = inverse_pivot(cond, heights, z, eigen[n], inv[n], face)
-                    part[n] = (height * f[i, k, tile, :] + face * part[n]) * inv[n]
-            for n, tile in enumerate(tiles):
-                to_low[i, tile, :] = part[n]
+            for tile in tiles:
+                _, part = leap(
+                    cond, heights, first, depth, eigen_of(i, tile), inv_high[i, tile, :],
+                    from_high[i, tile, :],
+                    lambda z: row(heights, z) * f[i, z - first, tile, :], False,
+                )
+                to_low[i, tile, :] = part
             down_copy(i).start()
+
+    def block_of(rank):
+        return rank // share
+
+    def ends_copy(off, owner, target):
+        return pltpu.make_async_remote_copy(
+            src_ref=ends.at[block_of(target)], dst_ref=ends_in.at[owner],
+            send_sem=sem_e.at[0, off], recv_sem=sem_e.at[1, off],
+            device_id=(growth, target), device_id_type=MESH,
+        )
+
+    def modal_copy(i):
+        return pltpu.make_async_copy(modal.at[i], modal_out.at[i], sem_m.at[i])
 
     def finish(i):
         face = row(cond, first + depth)
@@ -307,10 +332,15 @@
                     value[n] = part_s[i, k, tile, :] + (face * inv_s[i, k, tile, :]) * value[n]
             sums = []
             for n, tile in enumerate(tiles):
-                modal_out[i, k, tile, :] = value[n]
+                modal[i, k, tile, :] = value[n]
                 sums.append(jnp.sum(weight[n] * value[n], axis=0, keepdims=True))
             ends[i, k : k + 1, :] = sums[0] + sums[1]
             ends[i, depth + k : depth + k + 1, :] = sums[0] - sums[1]
+        modal_copy(i).start()
+        for n in range(share):
+            target = i * share + n
+            off = lax.rem(target + lanes_count - lat, lanes_count)
+            pl.when(target != lat)(ends_copy(off, lat, target).start)
 
     per_pair = PAIR // LANES
     cuts = lanes_count - 1
@@ -364,32 +394,8 @@
 
     lax.fori_loop(0, pl.cdiv(nblk + lag, per_pair), stage, 0)
 
-    def block_of(rank):
-        return rank // share
-
-    def ends_copy(off, owner, target):
-        return pltpu.make_async_remote_copy(
-            src_ref=ends.at[block_of(target)], dst_ref=ends_in.at[owner],
-            send_sem=sem_e.at[0, off], recv_sem=sem_e.at[1, off],
-            device_id=(growth, target), device_id_type=MESH,
-        )
-
-    for off in range(1, lanes_count):
-        ends_copy(off, lat, lax.rem(lat + off, lanes_count)).start()
     ends_in[lat] = ends[block_of(lat)]
 
-    def drain(i, carry):
-        @pl.when(growth < slabs - 1)
-        def _():
-            up_copy(i).wait_send()
-
-        @pl.when(growth > 0)
-        def _():
-            down_copy(i).wait_send()
-
-        return carry
-
-    lax.fori_loop(0, nblk, drain, 0)
     for off in range(1, lanes_count):
         copy = ends_copy(
             off, lax.rem(lat + lanes_count - off, lanes_count), lax.rem(lat + off, lanes_count)
@@ -513,6 +519,19 @@
         target = lax.rem(lat + off, lanes_count)
         speaks(lat, g_copy(off, lat, target).wait_send)
         speaks(owner, g_copy(off, owner, target).wait_recv)
+    def drain(i, carry):
+        @pl.when(growth < slabs - 1)
+        def _():
+            up_copy(i).wait_send()
+
+        @pl.when(growth > 0)
+        def _():
+            down_copy(i).wait_send()
+
+        modal_copy(i).wait()
+        return carry
+
+    lax.fori_loop(0, nblk, drain, 0)
     jump_out[...] = g_in[...]
 
 
@@ -531,7 +550,6 @@
     table = pltpu.make_async_copy(ty_in, ty, sem_in.at[pairs])
     table.start()
     half = m // 2
-    nz = slabs * depth
     tiles = [slice(0, half), slice(half, m)]
     first = growth * depth
     fill_conduct(heights, cond)
@@ -554,12 +572,19 @@
         def up(z, state):
             return advance(z, row(cond, z), state)
 
-        def down(k, state):
-            z = nz - 1 - k
-            return advance(z, row(cond, z + 1), state)
-
-        high = lax.fori_loop(0, nz - first - depth, down, (zero,) * 4)
-        state = lax.fori_loop(0, first, up, (zero,) * 4)
+        def outside(n, upward):
+            def right(z):
+                return row(heights, z) * jump[i, n, pl.ds(z, 1), :]
+
+            def one(q, state):
+                start = (q if upward else slabs - 1 - q) * depth
+                return leap(cond, heights, start, depth, eigen[n], *state, right, upward)
+
+            trips = growth if upward else slabs - 1 - growth
+            return lax.fori_loop(0, trips, one, (zero, zero))
+
+        high = outside(0, False) + outside(1, False)
+        state = outside(0, True) + outside(1, True)
         for k in range(depth):
             state = up(first + k, state)
             for n, tile in enumerate(tiles):
@@ -686,8 +711,9 @@
             jax.ShapeDtypeStruct((nz, LANES), f32),
         ),
         in_specs=[anywhere, smem, anywhere] + [vmem] * 4 + [anywhere],
-        out_specs=(vmem, vmem, vmem),
+        out_specs=(anywhere, vmem, vmem),
         scratch_shapes=[
+            V((nblk, depth, m, LANES), f32),
             V((depth * m, width), f32),
             V((depth, LANES), f32),
             V((2, 3 * mid, mid), jnp.bfloat16),
@@ -714,6 +740,7 @@
             V((lanes_count, 2, nz, LANES), f32),
             V((nblk, 2, nz, LANES), f32),
             dma((3,)),
+            dma((nblk,)),
             dma((2, slabs)),
             dma((2, nblk)),
             dma((2, nblk)),

time: 78.2 us -> 71.5 us (0.914)
  Pallas kernels: 78 us -> 71.3 us
    pallas_call x1, Pallas kernels: 57.2 us -> 53.2 us  [per_device(): pl.pallas_call(functools.partial(forward_kernel, slabs, lanes_count), out...]
    pallas_call x1, Pallas kernels: 20.8 us -> 18.1 us  [per_device(): pl.pallas_call(functools.partial(inverse_kernel, slabs), out_shape=jax.Sh...]
where the time goes in v4:
time: 71.5 us; the launch traced here: 71.3 us
  Pallas kernels  71.3 us (100%)
    pallas_call x1, Pallas kernels, per_device(): pl.pallas_call(functools.partial(forward_kernel, slabs, lanes_count), out...  53.2 us
    pallas_call x1, Pallas kernels, per_device(): pl.pallas_call(functools.partial(inverse_kernel, slabs), out_shape=jax.Sh...  18.1 us

profile of v4, /device:TPU:0, one launch (start us, length us, event | category | flops | bytes accessed | tf_op | source)
XLA Modules:
  0.0 71.3 jit_solution(82009106029690304)
XLA Ops:
  0.0 53.2 %slab_solve.1 = (f32[8,8,128,128]{3,2,1,0:T(8,128)}, f32[8,2,32,128]{3,2,1,0:T(8,128)}, f32[32,128]{1,0:T(8,128)}) custom-call(f32[1024,1024]{1,0:T(8,128)} %bitcast.2, f32[8]{0:T(128)} %spacing.1, bf16[2,1536,512]{2,1,0:T(8,128)(2,1)} %constant.16.clone.ty_in, bf16[128,384]{1,0:T(8,128)(2,1)} %constant.18.clone.tx, f32[128,128]{1,0:T(8,128)} %constant.20.clone.phi, ...), custom_call_target="tpu_custom_call" | custom-call | tf_op jit(solution)/shard_map/slab_solve/pallas_call | solution.py:706
  53.2 18.1 %face_correction.1 = f32[1024,1024]{1,0:T(8,128)} custom-call(f32[8,8,128,128]{3,2,1,0:T(8,128)} %get-tuple-element.8.modal_in, f32[8,2,32,128]{3,2,1,0:T(8,128)} %get-tuple-element.9.jump, f32[32,128]{1,0:T(8,128)} %get-tuple-element.10.heights, bf16[2,1536,512]{2,1,0:T(8,128)(2,1)} %constant.17.clone.ty_in, bf16[128,384]{1,0:T(8,128)(2,1)} %constant.19.clone.tx, ...), custom_call_target="tpu_custom_call" | custom-call | tf_op jit(solution)/shard_map/face_correction/pallas_call | solution.py:757

commit v5 on v4

--- a/solution.py
+++ b/solution.py
@@ -107,7 +107,7 @@
     modal_out, jump_out, heights_out,
     modal, src, spread, ty, lam, heights, cond, x3, f, inv_s, part_s, inv_high, from_low, from_high,
     to_low, to_high, ends, ends_in, jumps, jumps_all, k_inv, k_part, g_modes, g_cuts,
-    g_send, g_in, sem_in, sem_m, sem_h, sem_up, sem_down, sem_e, sem_r, sem_g,
+    g_send, g_in, sem_in, sem_m, sem_h, sem_up, sem_down, sem_e, sem_r, sem_j, sem_g,
 ):
     growth = lax.axis_index("growth")
     lat = lax.axis_index("lat")
@@ -119,11 +119,16 @@
     share = max(1, lanes_count // nblk)
     tiles = [slice(0, half), slice(half, m)]
     lag = LAG * (slabs - 1)
+    per_slab = lam.shape[0]
 
     loads = [
         pltpu.make_async_copy(a, b, sem_in.at[n])
         for n, (a, b) in enumerate(
-            [(src_in, src), (ty_in, ty), (lam_in, lam)]
+            [
+                (src_in, src),
+                (ty_in, ty),
+                (lam_in.at[pl.ds(growth * per_slab, per_slab)], lam),
+            ]
         )
     ]
     for load in loads:
@@ -174,16 +179,6 @@
         return carry
 
     lax.fori_loop(0, depth, split_rows, 0)
-    for off in range(1, slabs):
-        behind = lax.rem(growth + slabs - off, slabs)
-        copy = height_copy(off, behind, lax.rem(growth + off, slabs))
-        copy.wait_send()
-        copy.wait_recv()
-    fill_conduct(heights, cond)
-    heights_out[...] = heights[...]
-    for load in loads[1:]:
-        load.wait()
-
     def eigen_of(i, tile):
         at = pl.ds(pl.multiple_of(i * LANES, LANES), LANES)
         return lk[tile, :] + lb[:, at]
@@ -245,6 +240,17 @@
             return carry
 
         lax.fori_loop(0, rows // chunk, one, 0)
+
+    loads[1].wait()
+    transform(0)
+    for off in range(1, slabs):
+        behind = lax.rem(growth + slabs - off, slabs)
+        copy = height_copy(off, behind, lax.rem(growth + off, slabs))
+        copy.wait_send()
+        copy.wait_recv()
+    fill_conduct(heights, cond)
+    heights_out[...] = heights[...]
+    loads[2].wait()
 
     def up_copy(i):
         return pltpu.make_async_remote_copy(
@@ -345,7 +351,7 @@
     per_pair = PAIR // LANES
     cuts = lanes_count - 1
     middle = nz // 2
-    per_step = pl.cdiv(cuts, lag)
+    per_step = pl.cdiv(per_slab, lag)
 
     def face_pivots(j):
         weight = [lam[j, tile, :] for tile in tiles]
@@ -364,7 +370,7 @@
                 k_inv[j, z, tile, :] = high[n]
 
     def stage(tt, carry):
-        @pl.when(tt < nblk // per_pair)
+        @pl.when((tt > 0) & (tt < nblk // per_pair))
         def _():
             transform(tt)
 
@@ -376,7 +382,7 @@
 
             for n in range(per_step):
                 j = (t - nblk) * per_step + n
-                pl.when((j >= 0) & (j < cuts))(functools.partial(face_pivots, j))
+                pl.when((j >= 0) & (j < per_slab))(functools.partial(face_pivots, j))
 
             @pl.when((up_i >= 0) & (up_i < nblk))
             def _():
@@ -416,11 +422,17 @@
         for c in range(1, cuts):
             total += jump[c] * sines[c][j]
         jumps[j] = total
-    jumps_all[growth] = jumps[...]
+    for j in range(cuts, jumps.shape[0]):
+        jumps[j] = jnp.zeros(jumps.shape[1:], jnp.float32)
+
+    def share_of(rank):
+        return pl.ds(rank * per_slab, per_slab)
+
+    jumps_all[growth] = jumps[share_of(growth)]
 
     def jumps_copy(off, owner, target):
         return pltpu.make_async_remote_copy(
-            src_ref=jumps, dst_ref=jumps_all.at[owner],
+            src_ref=jumps.at[share_of(target)], dst_ref=jumps_all.at[owner],
             send_sem=sem_r.at[0, off], recv_sem=sem_r.at[1, off],
             device_id=(target, lat), device_id_type=MESH,
         )
@@ -457,7 +469,7 @@
             total = sum(
                 jnp.sum(w * v, axis=0, keepdims=True) for w, v in zip(weight, value)
             )
-            g_modes[j, z : z + 1, :] = held(z) - total * (1.0 / m)
+            g_modes[growth, j, z : z + 1, :] = held(z) - total * (1.0 / m)
 
         face = row(cond, middle)
         below, above = [], []
@@ -479,14 +491,27 @@
             for n, tile in enumerate(tiles):
                 above[n] = k_part[z, tile, :] + (face * k_inv[j, z, tile, :]) * above[n]
             put(z, above)
+        for off in range(1, slabs):
+            modes_copy(off, growth, j).start()
         return carry
 
-    lax.fori_loop(0, cuts, correct, 0)
+    def modes_copy(off, owner, j):
+        return pltpu.make_async_remote_copy(
+            src_ref=g_modes.at[owner, j], dst_ref=g_modes.at[owner, j],
+            send_sem=sem_j.at[0, off, j], recv_sem=sem_j.at[1, off, j],
+            device_id=(lax.rem(growth + off, slabs), lat), device_id_type=MESH,
+        )
+
+    lax.fori_loop(0, per_slab, correct, 0)
+    for off in range(1, slabs):
+        for j in range(per_slab):
+            modes_copy(off, growth, j).wait_send()
+            modes_copy(off, lax.rem(growth + slabs - off, slabs), j).wait_recv()
 
     for c in range(cuts):
-        total = g_modes[0] * sines[c][0]
+        total = g_modes[0, 0] * sines[c][0]
         for j in range(1, cuts):
-            total += g_modes[j] * sines[c][j]
+            total += g_modes[j // per_slab, j % per_slab] * sines[c][j]
         g_cuts[c] = total
     for d in range(lanes_count):
         low = g_cuts[d - 1] if d > 0 else jnp.zeros((nz, LANES), jnp.float32)
@@ -695,6 +720,8 @@
     for j in range(1, lanes_count):
         ids = [k for k in range(1, points) if k % (2 * lanes_count) in (j, 2 * lanes_count - j)]
         folds.append(eigenvalues(ids, points))
+    per_slab = pl.cdiv(cuts, slabs)
+    folds += [folds[0]] * (slabs * per_slab - cuts)
     lam = spread_lanes(np.stack(folds))
 
     flat = source.reshape(depth * m, width)
@@ -717,7 +744,7 @@
             V((depth * m, width), f32),
             V((depth, LANES), f32),
             V((2, 3 * mid, mid), jnp.bfloat16),
-            V((cuts, m, LANES), f32),
+            V((per_slab, m, LANES), f32),
             V((nz, LANES), f32),
             V((nz + 1, LANES), f32),
             V((2, depth * m, 3 * mid), jnp.bfloat16),
@@ -731,11 +758,11 @@
             V((nblk, m, LANES), f32),
             V((nblk, 2 * depth, LANES), f32),
             V((lanes_count, 2 * depth, LANES), f32),
-            V((cuts, depth, LANES), f32),
-            V((slabs, cuts, depth, LANES), f32),
-            V((cuts, nz, m, LANES), f32),
+            V((slabs * per_slab, depth, LANES), f32),
+            V((slabs, per_slab, depth, LANES), f32),
+            V((per_slab, nz, m, LANES), f32),
             V((nz, m, LANES), f32),
-            V((cuts, nz, LANES), f32),
+            V((slabs, per_slab, nz, LANES), f32),
             V((cuts, nz, LANES), f32),
             V((lanes_count, 2, nz, LANES), f32),
             V((nblk, 2, nz, LANES), f32),
@@ -746,6 +773,7 @@
             dma((2, nblk)),
             dma((2, lanes_count)),
             dma((2, slabs)),
+            dma((2, slabs, per_slab)),
             dma((2, lanes_count)),
         ],
         compiler_params=pltpu.CompilerParams(

time: 71.5 us -> 68.9 us (0.964)
  Pallas kernels: 71.3 us -> 68.7 us
    pallas_call x1, Pallas kernels: 53.2 us -> 50.6 us  [per_device(): pl.pallas_call(functools.partial(forward_kernel, slabs, lanes_count), out...]
where the time goes in v5:
time: 68.9 us; the launch traced here: 68.7 us
  Pallas kernels  68.7 us (100%)
    pallas_call x1, Pallas kernels, per_device(): pl.pallas_call(functools.partial(forward_kernel, slabs, lanes_count), out...  50.6 us
    pallas_call x1, Pallas kernels, per_device(): pl.pallas_call(functools.partial(inverse_kernel, slabs), out_shape=jax.Sh...  18.1 us

profile of v5, /device:TPU:0, one launch (start us, length us, event | category | flops | bytes accessed | tf_op | source)
XLA Modules:
  0.0 68.7 jit_solution(17288620187006687507)
XLA Ops:
  0.0 50.6 %slab_solve.1 = (f32[8,8,128,128]{3,2,1,0:T(8,128)}, f32[8,2,32,128]{3,2,1,0:T(8,128)}, f32[32,128]{1,0:T(8,128)}) custom-call(f32[1024,1024]{1,0:T(8,128)} %bitcast.2, f32[8]{0:T(128)} %spacing.1, bf16[2,1536,512]{2,1,0:T(8,128)(2,1)} %constant.16.clone.ty_in, bf16[128,384]{1,0:T(8,128)(2,1)} %constant.18.clone.tx, f32[128,128]{1,0:T(8,128)} %constant.20.clone.phi, ...), custom_call_target="tpu_custom_call" | custom-call | tf_op jit(solution)/shard_map/slab_solve/pallas_call | solution.py:733
  50.6 18.1 %face_correction.1 = f32[1024,1024]{1,0:T(8,128)} custom-call(f32[8,8,128,128]{3,2,1,0:T(8,128)} %get-tuple-element.8.modal_in, f32[8,2,32,128]{3,2,1,0:T(8,128)} %get-tuple-element.9.jump, f32[32,128]{1,0:T(8,128)} %get-tuple-element.10.heights, bf16[2,1536,512]{2,1,0:T(8,128)(2,1)} %constant.17.clone.ty_in, bf16[128,384]{1,0:T(8,128)(2,1)} %constant.19.clone.tx, ...), custom_call_target="tpu_custom_call" | custom-call | tf_op jit(solution)/shard_map/face_correction/pallas_call | solution.py:785

commit v6 on v5

--- a/solution.py
+++ b/solution.py
@@ -12,7 +12,7 @@
 
 LANES = 128
 PAIR = 256
-LAG = 2
+LAG = 3
 MESH = pl.DeviceIdType.MESH
 VMEM_BYTES = 56 * 1024 * 1024
 
@@ -579,7 +579,7 @@
     first = growth * depth
     fill_conduct(heights, cond)
 
-    def correct(i, side):
+    def correct(i, side, slot, jobs):
         at = pl.ds(pl.multiple_of(i * LANES, LANES), LANES)
         eigen = [lk[tile, :] + lb[:, at] for tile in tiles]
         zero = jnp.zeros((half, LANES), jnp.float32)
@@ -611,6 +611,8 @@
         high = outside(0, False) + outside(1, False)
         state = outside(0, True) + outside(1, True)
         for k in range(depth):
+            for job in jobs[k::depth]:
+                job()
             state = up(first + k, state)
             for n, tile in enumerate(tiles):
                 inv_s[k, tile, :] = state[2 * n]
@@ -631,31 +633,42 @@
                 columns = slice(side * LANES, (side + 1) * LANES)
                 for place, part in enumerate((a, a, b)):
                     start = place * m + n * half
-                    m3[k, start : start + half, columns] = part
-
-    def pair(tt, carry):
-        part = pl.ds(tt * per_pair, per_pair)
-        pltpu.make_async_copy(modal_in.at[part], modal.at[part], sem_in.at[tt]).wait()
-        for side in range(per_pair):
-            correct(tt * per_pair + side, side)
-        parity = tt // half_pairs
-        offset = lax.rem(tt, half_pairs) * PAIR
-        for k in range(depth):
-            a, b = split(dot(tx[...], m3[k]))
-            for place, part in enumerate((a, b, a)):
-                columns = pl.ds(pl.multiple_of(place * mid + offset, PAIR), PAIR)
-                g3[parity, k * m : (k + 1) * m, columns] = part
-        return carry
+                    m3[slot, k, start : start + half, columns] = part
 
     width = out.shape[1]
     mid = width // 2
     half_pairs = mid // PAIR
-
-    lax.fori_loop(0, pairs, pair, 0)
-    table.wait()
-
     rows = out.shape[0]
     chunk = min(256, rows)
+
+    def along_x(tt, k):
+        a, b = split(dot(tx[...], m3[tt % 2, k]))
+        for place, part in enumerate((a, b, a)):
+            start = place * mid + (tt % half_pairs) * PAIR
+            g3[tt // half_pairs, k * m : (k + 1) * m, start : start + PAIR] = part
+
+    def even_part(r, c):
+        at = slice(r * chunk, (r + 1) * chunk)
+        columns = slice(c * PAIR, (c + 1) * PAIR)
+        out[at, columns] = dot(g3[0, at, :], ty[0, :, columns])
+
+    for tt in range(pairs):
+        part = pl.ds(tt * per_pair, per_pair)
+        pltpu.make_async_copy(modal_in.at[part], modal.at[part], sem_in.at[tt]).wait()
+        jobs = []
+        if tt > 0:
+            jobs += [functools.partial(along_x, tt - 1, k) for k in range(depth)]
+        if tt == pairs - 1:
+            table.wait()
+            jobs += [
+                functools.partial(even_part, r, c)
+                for c in range(half_pairs)
+                for r in range(rows // chunk)
+            ]
+        for side in range(per_pair):
+            correct(tt * per_pair + side, side, tt % 2, jobs[side::per_pair])
+    for k in range(depth):
+        along_x(pairs - 1, k)
 
     def store(c, side):
         start = c * PAIR if side == 0 else width - (c + 1) * PAIR
@@ -669,7 +682,7 @@
 
         def rows_of(r, inner):
             at = pl.ds(pl.multiple_of(r * chunk, chunk), chunk)
-            even = dot(g3[0, at, :], ty[0, :, columns])
+            even = out[at, columns]
             odd = dot(g3[1, at, :], ty[1, :, columns])
             out[at, columns] = even + odd
             far = even - odd
@@ -796,7 +809,7 @@
             V((nz + 1, LANES), f32),
             V((depth, m, LANES), f32),
             V((depth, m, LANES), f32),
-            V((depth, 3 * m, PAIR), jnp.bfloat16),
+            V((2, depth, 3 * m, PAIR), jnp.bfloat16),
             V((2, depth * m, 3 * mid), jnp.bfloat16),
         ],
         compiler_params=pltpu.CompilerParams(vmem_limit_bytes=VMEM_BYTES),

time: 68.9 us -> 67.2 us (0.975)
  Pallas kernels: 68.7 us -> 66.8 us
    pallas_call x1, Pallas kernels: 50.6 us -> 49.3 us  [per_device(): pl.pallas_call(functools.partial(forward_kernel, slabs, lanes_count), out...]
where the time goes in v6:
time: 67.2 us; the launch traced here: 67 us
  Pallas kernels  66.8 us (99%)
    pallas_call x1, Pallas kernels, per_device(): pl.pallas_call(functools.partial(forward_kernel, slabs, lanes_count), out...  49.3 us
    pallas_call x1, Pallas kernels, per_device(): pl.pallas_call(functools.partial(inverse_kernel, slabs), out_shape=jax.Sh...  17.6 us

profile of v6, /device:TPU:0, one launch (start us, length us, event | category | flops | bytes accessed | tf_op | source)
XLA Modules:
  0.0 67.0 jit_solution(13663577803648364178)
XLA Ops:
  0.0 49.3 %slab_solve.1 = (f32[8,8,128,128]{3,2,1,0:T(8,128)}, f32[8,2,32,128]{3,2,1,0:T(8,128)}, f32[32,128]{1,0:T(8,128)}) custom-call(f32[1024,1024]{1,0:T(8,128)} %bitcast.2, f32[8]{0:T(128)} %spacing.1, bf16[2,1536,512]{2,1,0:T(8,128)(2,1)} %constant.16.clone.ty_in, bf16[128,384]{1,0:T(8,128)(2,1)} %constant.18.clone.tx, f32[128,128]{1,0:T(8,128)} %constant.20.clone.phi, ...), custom_call_target="tpu_custom_call" | custom-call | tf_op jit(solution)/shard_map/slab_solve/pallas_call | solution.py:746
  49.3 17.6 %face_correction.1 = f32[1024,1024]{1,0:T(8,128)} custom-call(f32[8,8,128,128]{3,2,1,0:T(8,128)} %get-tuple-element.8.modal_in, f32[8,2,32,128]{3,2,1,0:T(8,128)} %get-tuple-element.9.jump, f32[32,128]{1,0:T(8,128)} %get-tuple-element.10.heights, bf16[2,1536,512]{2,1,0:T(8,128)(2,1)} %constant.17.clone.ty_in, bf16[128,384]{1,0:T(8,128)(2,1)} %constant.19.clone.tx, ...), custom_call_target="tpu_custom_call" | custom-call | tf_op jit(solution)/shard_map/face_correction/pallas_call | solution.py:798

commit v7 on v6

--- a/solution.py
+++ b/solution.py
@@ -125,13 +125,18 @@
         pltpu.make_async_copy(a, b, sem_in.at[n])
         for n, (a, b) in enumerate(
             [
-                (src_in, src),
                 (ty_in, ty),
                 (lam_in.at[pl.ds(growth * per_slab, per_slab)], lam),
             ]
         )
     ]
-    for load in loads:
+    planes_in = [
+        pltpu.make_async_copy(
+            src_in.at[pl.ds(k * m, m)], src.at[pl.ds(k * m, m)], sem_in.at[2 + k]
+        )
+        for k in range(depth)
+    ]
+    for load in planes_in + loads:
         load.start()
     for k in range(depth):
         spread[k : k + 1, :] = jnp.full((1, LANES), spacing[k], jnp.float32)
@@ -146,28 +151,13 @@
             barrier, inc=1, device_id=(growth, lax.rem(lat + off, lanes_count)),
             device_id_type=MESH,
         )
-    pl.semaphore_wait(barrier, slabs + lanes_count - 2)
-
-    def height_copy(off, owner, target):
-        return pltpu.make_async_remote_copy(
-            src_ref=spread,
-            dst_ref=heights.at[pl.ds(owner * depth, depth)],
-            send_sem=sem_h.at[0, off],
-            recv_sem=sem_h.at[1, off],
-            device_id=(target, lat),
-            device_id_type=MESH,
-        )
-
-    for off in range(1, slabs):
-        height_copy(off, growth, lax.rem(growth + off, slabs)).start()
-    heights[pl.ds(growth * depth, depth), :] = spread[...]
     rows = src.shape[0]
-    loads[0].wait()
 
     mid = width // 2
 
     def split_rows(i, carry):
         at = pl.ds(pl.multiple_of(i * m, m), m)
+        pltpu.make_async_copy(src_in.at[at], src.at[at], sem_in.at[2 + i]).wait()
         for q in range(mid // LANES):
             near = src[at, q * LANES : (q + 1) * LANES]
             far = mirror(src[at, width - (q + 1) * LANES : width - q * LANES])
@@ -179,6 +169,21 @@
         return carry
 
     lax.fori_loop(0, depth, split_rows, 0)
+    pl.semaphore_wait(barrier, slabs + lanes_count - 2)
+
+    def height_copy(off, owner, target):
+        return pltpu.make_async_remote_copy(
+            src_ref=spread,
+            dst_ref=heights.at[pl.ds(owner * depth, depth)],
+            send_sem=sem_h.at[0, off],
+            recv_sem=sem_h.at[1, off],
+            device_id=(target, lat),
+            device_id_type=MESH,
+        )
+
+    for off in range(1, slabs):
+        height_copy(off, growth, lax.rem(growth + off, slabs)).start()
+    heights[pl.ds(growth * depth, depth), :] = spread[...]
     def eigen_of(i, tile):
         at = pl.ds(pl.multiple_of(i * LANES, LANES), LANES)
         return lk[tile, :] + lb[:, at]
@@ -241,7 +246,7 @@
 
         lax.fori_loop(0, rows // chunk, one, 0)
 
-    loads[1].wait()
+    loads[0].wait()
     transform(0)
     for off in range(1, slabs):
         behind = lax.rem(growth + slabs - off, slabs)
@@ -250,7 +255,7 @@
         copy.wait_recv()
     fill_conduct(heights, cond)
     heights_out[...] = heights[...]
-    loads[2].wait()
+    loads[1].wait()
 
     def up_copy(i):
         return pltpu.make_async_remote_copy(
@@ -670,36 +675,27 @@
     for k in range(depth):
         along_x(pairs - 1, k)
 
-    def store(c, side):
-        start = c * PAIR if side == 0 else width - (c + 1) * PAIR
-        columns = pl.ds(start if isinstance(c, int) else pl.multiple_of(start, PAIR), PAIR)
-        return pltpu.make_async_copy(
-            out.at[:, columns], out_hbm.at[:, columns], sem_out.at[2 * c + side]
-        )
-
-    def columns_of(c, carry):
-        columns = pl.ds(pl.multiple_of(c * PAIR, PAIR), PAIR)
-
-        def rows_of(r, inner):
-            at = pl.ds(pl.multiple_of(r * chunk, chunk), chunk)
+    def store(r):
+        at = pl.ds(r * chunk if isinstance(r, int) else pl.multiple_of(r * chunk, chunk), chunk)
+        return pltpu.make_async_copy(out.at[at], out_hbm.at[at], sem_out.at[r])
+
+    def rows_of(r, carry):
+        at = pl.ds(pl.multiple_of(r * chunk, chunk), chunk)
+        for c in range(half_pairs):
+            columns = slice(c * PAIR, (c + 1) * PAIR)
             even = out[at, columns]
             odd = dot(g3[1, at, :], ty[1, :, columns])
             out[at, columns] = even + odd
             far = even - odd
             for q in range(PAIR // LANES):
-                start = pl.multiple_of(width - c * PAIR - (q + 1) * LANES, LANES)
-                out[at, pl.ds(start, LANES)] = mirror(far[:, q * LANES : (q + 1) * LANES])
-            return inner
-
-        lax.fori_loop(0, rows // chunk, rows_of, 0)
-        for side in range(2):
-            store(c, side).start()
+                start = width - c * PAIR - (q + 1) * LANES
+                out[at, start : start + LANES] = mirror(far[:, q * LANES : (q + 1) * LANES])
+        store(r).start()
         return carry
 
-    lax.fori_loop(0, half_pairs, columns_of, 0)
-    for c in range(half_pairs):
-        for side in range(2):
-            store(c, side).wait()
+    lax.fori_loop(0, rows // chunk, rows_of, 0)
+    for r in range(rows // chunk):
+        store(r).wait()
 
 
 def per_device(source, spacing):
@@ -779,7 +775,7 @@
             V((cuts, nz, LANES), f32),
             V((lanes_count, 2, nz, LANES), f32),
             V((nblk, 2, nz, LANES), f32),
-            dma((3,)),
+            dma((depth + 2,)),
             dma((nblk,)),
             dma((2, slabs)),
             dma((2, nblk)),

time: 67.2 us -> 65.9 us (0.981)
  Pallas kernels: 66.8 us -> 65.5 us
    pallas_call x1, Pallas kernels: 17.6 us -> 16.4 us  [per_device(): pl.pallas_call(functools.partial(inverse_kernel, slabs), out_shape=jax.Sh...]
where the time goes in v7:
time: 65.9 us; the launch traced here: 65.7 us
  Pallas kernels  65.5 us (99%)
    pallas_call x1, Pallas kernels, per_device(): pl.pallas_call(functools.partial(forward_kernel, slabs, lanes_count), out...  49.2 us
    pallas_call x1, Pallas kernels, per_device(): pl.pallas_call(functools.partial(inverse_kernel, slabs), out_shape=jax.Sh...  16.4 us

profile of v7, /device:TPU:0, one launch (start us, length us, event | category | flops | bytes accessed | tf_op | source)
XLA Modules:
  0.0 65.7 jit_solution(2583089811533888292)
XLA Ops:
  0.0 49.2 %slab_solve.1 = (f32[8,8,128,128]{3,2,1,0:T(8,128)}, f32[8,2,32,128]{3,2,1,0:T(8,128)}, f32[32,128]{1,0:T(8,128)}) custom-call(f32[1024,1024]{1,0:T(8,128)} %bitcast.2, f32[8]{0:T(128)} %spacing.1, bf16[2,1536,512]{2,1,0:T(8,128)(2,1)} %constant.16.clone.ty_in, bf16[128,384]{1,0:T(8,128)(2,1)} %constant.18.clone.tx, f32[128,128]{1,0:T(8,128)} %constant.20.clone.phi, ...), custom_call_target="tpu_custom_call" | custom-call | tf_op jit(solution)/shard_map/slab_solve/pallas_call | solution.py:742
  49.2 16.4 %face_correction.1 = f32[1024,1024]{1,0:T(8,128)} custom-call(f32[8,8,128,128]{3,2,1,0:T(8,128)} %get-tuple-element.8.modal_in, f32[8,2,32,128]{3,2,1,0:T(8,128)} %get-tuple-element.9.jump, f32[32,128]{1,0:T(8,128)} %get-tuple-element.10.heights, bf16[2,1536,512]{2,1,0:T(8,128)(2,1)} %constant.17.clone.ty_in, bf16[128,384]{1,0:T(8,128)(2,1)} %constant.19.clone.tx, ...), custom_call_target="tpu_custom_call" | custom-call | tf_op jit(solution)/shard_map/face_correction/pallas_call | solution.py:794
